TPU v7x, 128 devices: a whole 4x4x4 slice. The times are simulated.
128 devices in a mesh: row: 8 (over x, core), col: 16 (over y, z).
Axes of the slice: x: 4, y: 4, z: 4, core: 2. Of those that a mesh axis runs over, the one named last changes fastest.
Arguments:
- block_input: bfloat16 [1536, 8192], P('col', 'row'), may hold values from -60 to 60
- modulation: float32 [8, 3, 8192], P(None, None, 'row'), may hold values from -3 to 3
- iteration: int32 [1], replicated, may hold values from 0 to 7
- positions: int32 [1536], replicated, may hold values from 0 to 1535, each once
- qkv_weight: bfloat16 [8192, 3, 8192], P('row', None, 'col'), may hold values from -2 to 2
- out_weight: bfloat16 [8192, 8192], P('col', 'row'), may hold values from -0.0625 to 0.0625
- grad_out: bfloat16 [1536, 8192], P('col', 'row'), may hold values from -6 to 6
Outputs:
- grad_input: bfloat16 [1536, 8192], P('col', 'row')
- grad_qkv: bfloat16 [8192, 3, 8192], P('row', None, 'col')
- grad_out_weight: bfloat16 [8192, 8192], P('col', 'row')
- grad_mod: float32 [3, 8192], P(None, 'row')
Inputs may be any that keep to these rules, and one draw needn't show every extreme that they name: positions is a permutation of 0 to 1535.
All inputs are finite; a program needn't handle non-finite values.
Results may differ from a plain program's by a relative error of at most 0.0077.
Values may be sent and summed in bfloat16 or wider, within the bound.
A program may use at most 128 MiB of HBM per device.

v0:
```python
import jax
import jax.numpy as jnp
from jax import lax
from jax.sharding import PartitionSpec as P

D = 8192
HEAD_DIM = 128


EPS = 1e-06


def contract_rows(left, right):
    return lax.dot_general(
        left, right, (((0,), (0,)), ((), ())), preferred_element_type=jnp.float32
    )


def contract_cols(left, right):
    return lax.dot_general(
        left, right, (((1,), (1,)), ((), ())), preferred_element_type=jnp.float32
    )


def shards(block_input, modulation, iteration, positions, qkv_weight, out_weight, grad_out):
    row_count = lax.axis_size("row")
    col_count = lax.axis_size("col")
    tok_col, width_row = block_input.shape
    width_col = qkv_weight.shape[2]
    tokens = tok_col * col_count
    tok_row = tokens // row_count
    factor = 1.0 / HEAD_DIM**0.5
    chosen = lax.dynamic_index_in_dim(modulation, iteration[0], 0, keepdims=False)
    shift, scale, gate = (chosen[0], chosen[1], chosen[2])
    x_float = block_input.astype(jnp.float32)
    squares = lax.psum(jnp.sum(x_float * x_float, axis=1), "row")
    inv_rms = lax.rsqrt(squares / D + EPS)
    x_hat = x_float * inv_rms[:, None]
    normed = (x_hat * (1.0 + scale) + shift).astype(jnp.bfloat16)
    normed_full, grad_full = (
        lax.all_gather(normed, "col", axis=0, tiled=True),
        lax.all_gather(grad_out, "col", axis=0, tiled=True),
    )
    w_flat = qkv_weight.reshape(width_row, 3 * width_col)
    panel = normed_full
    qkv = lax.psum_scatter(
        jnp.dot(panel, w_flat, preferred_element_type=jnp.float32),
        "row",
        scatter_dimension=0,
        tiled=True,
    ).astype(jnp.bfloat16)
    query = qkv[:, :width_col]
    keys, values = (
        lax.all_gather(qkv[:, width_col : 2 * width_col], "row", axis=0, tiled=True),
        lax.all_gather(qkv[:, 2 * width_col :], "row", axis=0, tiled=True),
    )
    grad_float = grad_full.astype(jnp.float32)
    grad_z = (grad_float * gate).astype(jnp.bfloat16)
    panel = grad_z
    grad_ctx = lax.psum_scatter(
        contract_cols(panel, out_weight), "row", scatter_dimension=0, tiled=True
    ).astype(jnp.bfloat16)
    row_start = lax.axis_index("row") * tok_row
    query_pos = lax.dynamic_slice_in_dim(positions, row_start, tok_row, 0)
    allowed = positions[None, :] <= query_pos[:, None]
    heads_local = width_col // HEAD_DIM
    q_heads = query.reshape(tok_row, heads_local, HEAD_DIM)
    k_heads = keys.reshape(tokens, heads_local, HEAD_DIM)
    v_heads = values.reshape(tokens, heads_local, HEAD_DIM)
    g_heads = grad_ctx.reshape(tok_row, heads_local, HEAD_DIM)
    scores = (
        jnp.einsum("qhd,khd->hqk", q_heads, k_heads, preferred_element_type=jnp.float32) * factor
    )
    scores = jnp.where(allowed[None, :, :], scores, -1e30)
    peak = jnp.max(scores, axis=2, keepdims=True)
    weights = jnp.exp(scores - peak)
    probs = weights / jnp.sum(weights, axis=2, keepdims=True)
    probs_b = probs.astype(jnp.bfloat16)
    context = jnp.einsum("hqk,khd->qhd", probs_b, v_heads, preferred_element_type=jnp.float32)
    context = context.astype(jnp.bfloat16).reshape(tok_row, width_col)
    grad_probs = jnp.einsum("qhd,khd->hqk", g_heads, v_heads, preferred_element_type=jnp.float32)
    delta = jnp.sum(probs * grad_probs, axis=2, keepdims=True)
    grad_scores = (probs * (grad_probs - delta) * factor).astype(jnp.bfloat16)
    grad_query = jnp.einsum(
        "hqk,khd->qhd", grad_scores, k_heads, preferred_element_type=jnp.float32
    )
    grad_query = grad_query.astype(jnp.bfloat16).reshape(tok_row, width_col)
    grad_keys = jnp.einsum("hqk,qhd->khd", grad_scores, q_heads, preferred_element_type=jnp.float32)
    grad_values = jnp.einsum("hqk,qhd->khd", probs_b, g_heads, preferred_element_type=jnp.float32)
    kv_grad_term = jnp.concatenate(
        [grad_keys.reshape(tokens, width_col), grad_values.reshape(tokens, width_col)], axis=1
    )
    context_full = lax.all_gather(context, "row", axis=0, tiled=True)
    z_part = jnp.dot(context_full, out_weight, preferred_element_type=jnp.float32)
    gate_part = jnp.sum(grad_float * z_part, axis=0)
    gate_grad = lax.psum(gate_part, "col")
    grad_out_weight = contract_rows(context_full, grad_z).astype(jnp.bfloat16)
    kv_grad = lax.psum_scatter(kv_grad_term, "row", scatter_dimension=0, tiled=True).astype(
        jnp.bfloat16
    )
    local_grad = jnp.concatenate([grad_query, kv_grad], axis=1)
    grad_proj = lax.all_gather(local_grad, "row", axis=0, tiled=True)
    grad_qkv = (
        contract_rows(normed_full, grad_proj).astype(jnp.bfloat16).reshape(width_row, 3, width_col)
    )
    panel = grad_proj
    grad_normed = lax.psum_scatter(
        contract_cols(panel, w_flat), "col", scatter_dimension=0, tiled=True
    )
    shift_part = jnp.sum(grad_normed, axis=0)
    scale_part = jnp.sum(grad_normed * x_hat, axis=0)
    shift_grad, scale_grad = lax.psum((shift_part, scale_part), "col")
    grad_hat = grad_normed * (1.0 + scale)
    inner = lax.psum(jnp.sum(grad_hat * x_hat, axis=1), "row") / D
    own_grad = grad_out.astype(jnp.float32)
    grad_input = ((grad_hat - x_hat * inner[:, None]) * inv_rms[:, None] + own_grad).astype(
        jnp.bfloat16
    )
    grad_mod = jnp.stack([shift_grad, scale_grad, gate_grad], axis=0)
    return (grad_input, grad_qkv, grad_out_weight, grad_mod)


def solution(mesh):
    placed = (
        P("col", "row"),
        P(None, None, "row"),
        P(),
        P(),
        P("row", None, "col"),
        P("col", "row"),
        P("col", "row"),
    )
    return jax.shard_map(
        shards,
        mesh=mesh,
        in_specs=placed,
        out_specs=(P("col", "row"), P("row", None, "col"), P("col", "row"), P(None, "row")),
        check_vma=False,
    )
```

profile of v0, /device:TPU:0, one launch (start us, length us, event | category | flops | bytes accessed | tf_op | source)
XLA Modules:
  0.0 590.9 jit_solution(17754243266450543058)
XLA Ops:
  9.0 14.7 %psum.35 = f32[96]{0:T(128)S(1)} all-reduce(f32[96]{0:T(128)S(1)} %fusion.72), channel_id=1, replica_groups=mesh['row'=8,'col'=16] {'row'}, use_global_device_ids=true, to_apply=%region_1.2 | all-reduce | flops 96 | bytes 768 | tf_op jit(solution)/shard_map/psum | solution.py:36
  31.7 42.8 %all-gather.7.cloned.1.call-done = bf16[1536,1024]{1,0:T(8,128)(2,1)} async-done(((bf16[96,1024]{1,0:T(8,128)(2,1)}), bf16[1536,1024]{1,0:T(8,128)(2,1)}) %all-gather.7.cloned.1.call-update) | async-done | bytes 3145744 | tf_op jit(solution)/shard_map/all_gather | solution.py:41
  74.5 10.1 %fusion.105 = f32[1536,1536]{1,0:T(8,128)} fusion(bf16[1536,1024]{1,0:T(8,128)(2,1)} %all-gather.7.cloned.1.call-done, bf16[1024,1536]{0,1:T(8,128)(2,1)} %bitcast.105), kind=kOutput, calls=%fused_computation.87 | convolution fusion | flops 4831838208 | bytes 15728640 | tf_op jit(solution)/shard_map/dot_general | solution.py:47
  84.7 39.0 %all-gather.11.cloned.1.call-done = bf16[1536,1024]{1,0:T(8,128)(2,1)} async-done(((bf16[96,1024]{1,0:T(8,128)(2,1)}), bf16[1536,1024]{1,0:T(8,128)(2,1)}) %all-gather.11.cloned.1.call-update) | async-done | bytes 3145744 | tf_op jit(solution)/shard_map/all_gather | solution.py:42
  123.6 5.5 fusion.10
  129.2 53.0 %reduce-scatter.7.cloned.1.call-done = f32[192,1536]{1,0:T(8,128)} async-done(((f32[1536,1536]{1,0:T(8,128)}), f32[192,1536]{1,0:T(8,128)}) %reduce-scatter.7.cloned.1.call-update) | async-done | bytes 1179664 | tf_op jit(solution)/shard_map/reduce_scatter | solution.py:46
  185.5 34.3 %reduce-scatter.9.cloned.1.call-done = f32[192,512]{1,0:T(8,128)} async-done(((f32[1536,512]{1,0:T(8,128)}), f32[192,512]{1,0:T(8,128)}) %reduce-scatter.9.cloned.1.call-update) | async-done | bytes 393232 | tf_op jit(solution)/shard_map/reduce_scatter | solution.py:60
  219.8 25.5 %all-gather.13.cloned.1.call-done = bf16[1536,512]{1,0:T(8,128)(2,1)} async-done(((bf16[192,512]{1,0:T(8,128)(2,1)}), bf16[1536,512]{1,0:T(8,128)(2,1)}) %all-gather.13.cloned.1.call-update) | async-done | bytes 1572880 | tf_op jit(solution)/shard_map/all_gather | solution.py:55
  249.7 22.4 %all-gather.9.cloned.1.call-done = bf16[1536,512]{1,0:T(8,128)(2,1)} async-done(((bf16[192,512]{1,0:T(8,128)(2,1)}), bf16[1536,512]{1,0:T(8,128)(2,1)}) %all-gather.9.cloned.1.call-update) | async-done | bytes 1572880 | tf_op jit(solution)/shard_map/all_gather | solution.py:54
  272.1 5.3 fusion.100
  277.5 12.7 %fusion.13 = f32[4,128,1536]{2,1,0:T(8,128)} fusion(f32[4,192,1536]{2,1,0:T(8,128)} %fusion.25, bf16[24,4,8,128]{3,2,1,0:T(8,128)(2,1)S(1)} %get-tuple-element.23, f32[4,192,1536]{2,1,0:T(8,128)} %get-tuple-element.29, f32[4,192]{1,0:T(4,128)S(1)} %get-tuple-element.28), kind=kOutput, calls=%fused_computation.16 | convolution fusion | flops 310249728 | bytes 12782592 | tf_op jit(solution)/shard_map/hqk,qhd->khd/dot_general | solution.py:88
  296.6 6.6 %copy.50 = f32[1536,1024]{1,0:T(8,128)} copy(f32[1536,1024]{0,1:T(8,128)} %pad_maximum_fusion) | data formatting | bytes 12582912
  303.2 11.0 %fusion.50 = bf16[192,4,128]{2,0,1:T(8,128)(2,1)S(1)} fusion(f32[4,192,1536]{2,1,0:T(8,128)} %fusion.25, f32[4,192,1536]{2,1,0:T(8,128)} %get-tuple-element.29, f32[4,192]{1,0:T(4,128)S(1)} %get-tuple-element.28, bf16[1536,512]{1,0:T(8,128)(2,1)} %all-gather.9.cloned.1.call-done), kind=kOutput, calls=%fused_computation.41 | convolution fusion | flops 310348032 | bytes 11209728 | tf_op jit(solution)/shard_map/hqk,khd->qhd/dot_general | solution.py:84
  314.4 31.7 %reduce-scatter.13.cloned.1.call-done = f32[192,1024]{1,0:T(8,128)} async-done(((f32[1536,1024]{1,0:T(8,128)}), f32[192,1024]{1,0:T(8,128)}) %reduce-scatter.13.cloned.1.call-update) | async-done | bytes 786448
  353.4 29.4 %all-gather.15.cloned.1.call-done = bf16[1536,1536]{1,0:T(8,128)(2,1)} async-done(((bf16[192,1536]{1,0:T(8,128)(2,1)}), bf16[1536,1536]{1,0:T(8,128)(2,1)}) %all-gather.15.cloned.1.call-update) | async-done | bytes 4718608 | tf_op jit(solution)/shard_map/all_gather | solution.py:102
  382.8 9.7 %fusion.106 = f32[1536,1024]{1,0:T(8,128)} fusion(bf16[1536,1536]{1,0:T(8,128)(2,1)} %all-gather.15.cloned.1.call-done, bf16[1024,1536]{0,1:T(8,128)(2,1)} %bitcast.106), kind=kOutput, calls=%fused_computation.88 | convolution fusion | flops 4831838208 | bytes 14155776 | tf_op jit(solution)/shard_map/dot_general | solution.py:20
  392.6 17.0 %all-gather.17.cloned.1.call-done = bf16[1536,512]{1,0:T(8,128)(2,1)} async-done(((bf16[192,512]{1,0:T(8,128)(2,1)}), bf16[1536,512]{1,0:T(8,128)(2,1)}) %all-gather.17.cloned.1.call-update) | async-done | bytes 1572880 | tf_op jit(solution)/shard_map/all_gather | solution.py:93
  409.6 5.3 fusion.30
  418.9 6.7 %convolution_convert_fusion = bf16[1024,1536]{1,0:T(8,128)(2,1)} fusion(bf16[1536,1024]{1,0:T(8,128)(2,1)S(1)} %copy-done.6, bf16[1536,1536]{1,0:T(8,128)(2,1)S(1)} %bitcast.121), kind=kOutput, calls=%fused_computation.13 | convolution fusion | flops 4833411072 | bytes 11010048 | tf_op jit(solution)/shard_map/dot_general | solution.py:14
  425.6 4.7 copy.45
  430.3 4.7 copy.48
  435.0 59.8 %reduce-scatter.11.cloned.1.call-done = f32[96,1024]{1,0:T(8,128)} async-done(((f32[1536,1024]{1,0:T(8,128)}), f32[96,1024]{1,0:T(8,128)}) %reduce-scatter.11.cloned.1.call-update) | async-done | bytes 393232 | tf_op jit(solution)/shard_map/reduce_scatter | solution.py:107
  496.0 13.5 %psum.36 = f32[96]{0:T(128)S(1)} all-reduce(f32[96]{0:T(128)S(1)} %get-tuple-element.17), channel_id=1, replica_groups=mesh['row'=8,'col'=16] {'row'}, use_global_device_ids=true, to_apply=%region_10.11 | all-reduce | flops 96 | bytes 768 | tf_op jit(solution)/shard_map/psum | solution.py:114
  509.5 72.1 %all-reduce = (f32[1,1024]{1,0:T(1,128)S(1)}, f32[1,1024]{1,0:T(1,128)S(1)}, f32[1,1024]{1,0:T(1,128)S(1)}) all-reduce(f32[1,1024]{1,0:T(1,128)S(1)} %bitcast.119, f32[1,1024]{1,0:T(1,128)S(1)} %bitcast.114, f32[1,1024]{1,0:T(1,128)S(1)} %bitcast.115), channel_id=1, replica_groups=mesh['row'=8,'col'=16] {'col'}, use_global_device_ids=true, to_apply=%region_16.17 | all-reduce | flops 3072 | bytes 24576 | tf_op jit(solution)/shard_map/psum | solution.py:96
  (64 shorter events, 38.5 us)
Async XLA Ops:
  7.2 116.4 %copy-start = (bf16[512,1024]{1,0:T(8,128)(2,1)S(1)}, bf16[512,1024]{1,0:T(8,128)(2,1)}, u32[]{:S(2)}) copy-start(bf16[512,1024]{1,0:T(8,128)(2,1)} %param.12) | copy-start | bytes 3145732
  7.2 67.3 %all-gather.7.cloned.1.call-start = ((), (), s32[]{:S(2)}) async-start(), calls=%async_computation.4 | async-start | bytes 3342336 | tf_op jit(solution)/shard_map/all_gather | solution.py:41
  26.3 97.3 %all-gather.11.cloned.1.call-start = ((), (), s32[]{:S(2)}) async-start(), calls=%async_computation.7 | async-start | bytes 3342336 | tf_op jit(solution)/shard_map/all_gather | solution.py:42
  27.0 155.2 %reduce-scatter.7.cloned.1.call-start = ((), (), s32[]{:S(2)}) async-start(), calls=%async_computation.5 | async-start | bytes 10616832 | tf_op jit(solution)/shard_map/reduce_scatter | solution.py:46
  84.6 135.2 %reduce-scatter.9.cloned.1.call-start = ((), (), s32[]{:S(2)}) async-start(), calls=%async_computation.8 | async-start | bytes 3538944 | tf_op jit(solution)/shard_map/reduce_scatter | solution.py:60
  129.1 56.1 %copy-start.5 = (s32[1536]{0:T(1024)S(1)}, s32[1536]{0:T(1024)}, u32[]{:S(2)}) copy-start(s32[1536]{0:T(1024)} %param.10) | copy-start | bytes 18436
  129.1 116.2 %all-gather.13.cloned.1.call-start = ((), (), s32[]{:S(2)}) async-start(), calls=%async_computation.9 | async-start | bytes 1769472 | tf_op jit(solution)/shard_map/all_gather | solution.py:55
  184.4 87.8 %all-gather.9.cloned.1.call-start = ((), (), s32[]{:S(2)}) async-start(), calls=%async_computation.6 | async-start | bytes 1769472 | tf_op jit(solution)/shard_map/all_gather | solution.py:54
  184.9 161.1 %reduce-scatter.13.cloned.1.call-start = ((), (), s32[]{:S(2)}) async-start(), calls=%async_computation.13 | async-start | bytes 7077888
  277.5 12.7 %copy-start.4 = (f32[192,512]{1,0:T(8,128)S(1)}, f32[192,512]{1,0:T(8,128)}, u32[]{:S(2)}) copy-start(f32[192,512]{1,0:T(8,128)} %reduce-scatter.9.cloned.1.call-done) | copy-start | bytes 1179652
  290.1 3.3 copy-start.2
  303.2 79.6 %all-gather.15.cloned.1.call-start = ((), (), s32[]{:S(2)}) async-start(), calls=%async_computation.10 | async-start | bytes 5308416 | tf_op jit(solution)/shard_map/all_gather | solution.py:102
  348.6 60.9 %all-gather.17.cloned.1.call-start = ((), (), s32[]{:S(2)}) async-start(), calls=%async_computation.12 | async-start | bytes 1769472 | tf_op jit(solution)/shard_map/all_gather | solution.py:93
  353.1 141.6 %reduce-scatter.11.cloned.1.call-start = ((), (), s32[]{:S(2)}) async-start(), calls=%async_computation.11 | async-start | bytes 6684672 | tf_op jit(solution)/shard_map/reduce_scatter | solution.py:107
  409.6 5.3 copy-start.7
  409.6 9.2 %slice-start = ((s8[4718592]{0:T(1024)(128)(4,1)}), s8[4194304]{0:T(1024)(128)(4,1)S(1)}, s32[]{:S(2)}) async-start(s8[4718592]{0:T(1024)(128)(4,1)} %bitcast.120), calls=%async_computation.14 | async-start | bytes 8388608
  414.9 3.9 slice-start.1
  414.9 4.0 copy-start.6
  430.3 64.5 %copy-start.1 = (bf16[96,1024]{1,0:T(8,128)(2,1)S(1)}, bf16[96,1024]{1,0:T(8,128)(2,1)}, u32[]{:S(2)}) copy-start(bf16[96,1024]{1,0:T(8,128)(2,1)} %param.7) | copy-start | bytes 589828
  430.3 151.9 %copy-start.3 = (bf16[96,1024]{1,0:T(8,128)(2,1)S(1)}, bf16[96,1024]{1,0:T(8,128)(2,1)}, u32[]{:S(2)}) copy-start(bf16[96,1024]{1,0:T(8,128)(2,1)} %param.13) | copy-start | bytes 589828
Sparse Core Ops, SparseCore 0:
  26.4 48.0 all-gather.6
  76.7 46.8 all-gather.10
  126.0 56.1 reduce-scatter.6
  184.5 35.2 reduce-scatter.8
  221.9 23.3 all-gather.12
  247.4 24.6 all-gather.8
  303.3 42.7 reduce-scatter.12
  348.8 33.9 all-gather.14
  385.1 24.4 all-gather.16
  412.8 81.8 reduce-scatter.10
where the time goes:
time: 592 us; the launch traced here: 591 us
  waiting for transfers between devices  356 us (60%)
  blocking collectives  100 us (17%)
  matrix products  81.6 us (14%)
  local copies, waits for them, and re-layouts  24.9 us (4%)
  between operations  15 us (3%)
  other arithmetic  12.2 us (2%)
    psum x1, blocking collectives, shards(): gate_grad = lax.psum(gate_part, 'col')  72.1 us
    reduce_scatter x1, waiting for transfers between devices, shards(): lax.psum_scatter(contract_cols(panel, w_flat), 'col', scatter_dimension=0...  59.8 us
    reduce_scatter x1, waiting for transfers between devices, shards(): lax.psum_scatter(jnp.dot(panel, w_flat, preferred_element_type=jnp.float3...  53 us
    all_gather x1, waiting for transfers between devices, shards(): lax.all_gather(normed, 'col', axis=0, tiled=True)  42.8 us
    all_gather x1, waiting for transfers between devices, shards(): lax.all_gather(grad_out, 'col', axis=0, tiled=True)  39 us
    reduce_scatter x1, waiting for transfers between devices, shards(): lax.psum_scatter(contract_cols(panel, out_weight), 'row', scatter_dimensi...  34.3 us
    unnamed x11, waiting for transfers between devices  33 us
    all_gather x1, waiting for transfers between devices, shards(): grad_proj = lax.all_gather(local_grad, 'row', axis=0, tiled=True)  29.4 us
  transfers between devices with their start and end apart: 10, of which 10 were waited for; matrix products, arithmetic and copies ran while one was open for 13% of the time, Pallas kernels for 0%

commit v1 on v0

v1 whole, which is shorter than its diff:
```python
import functools
import jax
import jax.numpy as jnp
from jax import lax
from jax.experimental import pallas as pl
from jax.experimental.pallas import tpu as pltpu
from jax.sharding import PartitionSpec as P

D = 8192
HEAD_DIM = 128
EPS = 1e-06
MESH = pl.DeviceIdType.MESH
BF = jnp.bfloat16
F32 = jnp.float32

CORE = (0, 1, 0, 0)
XP, XM, X2 = (1, 0, 0, 0), (3, 0, 0, 0), (2, 0, 0, 0)
YP, YM, Y2 = (0, 0, 1, 0), (0, 0, 3, 0), (0, 0, 2, 0)
ZP, ZM, Z2 = (0, 0, 0, 1), (0, 0, 0, 3), (0, 0, 0, 2)

G = 4
HALF = 192
F0, F1 = pl.ds(0, 512), pl.ds(512, 512)


def coords():
    row, col = lax.axis_index("row"), lax.axis_index("col")
    return row // 2, row % 2, col // 4, col % 4


def device(step):
    x, k, y, z = coords()
    dx, dk, dy, dz = step
    x, k, y, z = (x + dx) % 4, (k + dk) % 2, (y + dy) % 4, (z + dz) % 4
    return (x * 2 + k, y * 4 + z)


def enter(steps):
    barrier = pltpu.get_barrier_semaphore()
    for step in steps:
        pl.semaphore_signal(barrier, inc=1, device_id=device(step), device_id_type=MESH)
    pl.semaphore_wait(barrier, len(steps))


class Net:
    def __init__(self, send_sem, recv_sem):
        self.send_sem, self.recv_sem, self.copies = send_sem, recv_sem, []

    def send(self, src, dst, step):
        i = len(self.copies)
        copy = pltpu.make_async_remote_copy(
            src_ref=src,
            dst_ref=dst,
            send_sem=self.send_sem.at[i],
            recv_sem=self.recv_sem.at[i],
            device_id=device(step),
            device_id_type=MESH,
        )
        copy.start()
        self.copies.append(copy)
        return copy

    def drain(self):
        for copy in self.copies:
            copy.wait_send()


class Gather:
    def __init__(self, net, buf):
        _, _, y, z = coords()
        self.net, self.buf, self.y, self.z = net, buf, y, z
        self.yp, self.ym, self.y2 = (y + 1) % 4, (y + 3) % 4, (y + 2) % 4
        self.zp, self.zm, self.z2 = (z + 1) % 4, (z + 3) % 4, (z + 2) % 4
        self.first, self.second = {}, {}

    def put(self, ref, step):
        return self.net.send(ref, ref, step)

    def zsend(self, key, g):
        block = self.buf.at[g, self.z, :, F0]
        self.first[key] = (self.put(block, ZP), self.put(block, ZM))

    def zforward(self, key, g):
        up, down = self.first[key]
        up.wait_recv()
        a = self.put(self.buf.at[g, self.zm, pl.ds(0, 48), F0], ZP)
        down.wait_recv()
        b = self.put(self.buf.at[g, self.zp, pl.ds(48, 48), F0], ZM)
        self.second[key] = (a, b)

    def zend(self, key):
        a, b = self.second[key]
        a.wait_recv()
        b.wait_recv()

    def s1(self):
        f0, f1 = self.buf.at[self.y, self.z, :, F0], self.buf.at[self.y, self.z, :, F1]
        self.a, self.b = self.put(f0, YP), self.put(f0, YM)
        self.c, self.d = self.put(f1, ZP), self.put(f1, ZM)
        self.zsend("own", self.y)

    def s2(self):
        self.c.wait_recv()
        self.c2 = self.put(self.buf.at[self.y, self.zm, pl.ds(0, 48), F1], ZP)
        self.d.wait_recv()
        self.d2 = self.put(self.buf.at[self.y, self.zp, pl.ds(48, 48), F1], ZM)
        self.a.wait_recv()
        self.a2 = self.put(self.buf.at[self.ym, self.z, pl.ds(0, 48), F0], YP)
        self.zsend("ym", self.ym)
        self.b.wait_recv()
        self.b2 = self.put(self.buf.at[self.yp, self.z, pl.ds(48, 48), F0], YM)
        self.zsend("yp", self.yp)

    def s3(self):
        self.c2.wait_recv()
        self.d2.wait_recv()
        group = self.buf.at[self.y, :, :, F1]
        self.gp, self.gm = self.put(group, YP), self.put(group, YM)
        self.zforward("own", self.y)
        self.zend("own")

    def s4(self):
        self.a2.wait_recv()
        self.b2.wait_recv()
        self.zsend("y2", self.y2)
        self.zforward("ym", self.ym)
        self.zforward("yp", self.yp)
        self.gp.wait_recv()
        self.gp2 = self.put(self.buf.at[self.ym, pl.ds(0, 2), :, F1], YP)
        self.gm.wait_recv()
        self.gm2 = self.put(self.buf.at[self.yp, pl.ds(2, 2), :, F1], YM)
        self.zend("ym")
        self.zend("yp")

    def s5(self):
        self.zforward("y2", self.y2)
        self.zend("y2")
        self.gp2.wait_recv()
        self.gm2.wait_recv()


class RowReduce:
    def __init__(self, net, part, sib, hop, hop_in, out_buf, in_buf, w):
        self.net, self.part, self.sib, self.hop, self.hop_in = net, part, sib, hop, hop_in
        self.out_buf, self.in_buf, self.w = out_buf, in_buf, w
        self.x, self.k, _, _ = coords()
        self.c, self.h, self.f = {}, {}, {}

    def start(self, s):
        self.c[s] = self.net.send(self.part.at[s, 1 - self.k], self.sib.at[s], CORE)

    def local(self, s, d, rows):
        cols = pl.ds(d * self.w, self.w)
        return self.part[s, self.k, rows, cols].astype(F32) + self.sib[s, rows, cols].astype(F32)

    def r1(self, s):
        self.c[s].wait_recv()
        self.hop[s] = self.local(s, 0, pl.ds(0, HALF)).astype(BF)
        self.h[s] = (
            self.net.send(self.hop.at[s, pl.ds(0, 96)], self.hop_in.at[s, 0], XP),
            self.net.send(self.hop.at[s, pl.ds(96, 96)], self.hop_in.at[s, 1], XM),
        )

    def r2(self, s):
        a, b = self.h[s]
        lo, hi = pl.ds(0, 96), pl.ds(96, 96)
        self.out_buf[s, 0, hi] = self.local(s, 1, hi).astype(BF)
        self.out_buf[s, 1, lo] = self.local(s, 2, lo).astype(BF)
        a.wait_recv()
        self.out_buf[s, 0, lo] = (self.local(s, 1, lo) + self.hop_in[s, 0].astype(F32)).astype(BF)
        up = self.net.send(self.out_buf.at[s, 0], self.in_buf.at[s, 0], XP)
        b.wait_recv()
        self.out_buf[s, 1, hi] = (self.local(s, 2, hi) + self.hop_in[s, 1].astype(F32)).astype(BF)
        down = self.net.send(self.out_buf.at[s, 1], self.in_buf.at[s, 1], XM)
        self.f[s] = (up, down)

    def r3(self, s):
        own = self.local(s, 3, pl.ds(0, HALF))
        for copy in self.f[s]:
            copy.wait_recv()
        return (own + self.in_buf[s, 0].astype(F32) + self.in_buf[s, 1].astype(F32)).astype(BF)


def row_sum(net, mine, got, value):
    mine[0] = jnp.broadcast_to(value, (96, 128))
    net.send(mine.at[0], got.at[0], CORE).wait_recv()
    mine[1] = mine[0] + got[0]
    copies = [net.send(mine.at[1], got.at[1 + i], step) for i, step in enumerate((XP, XM, X2))]
    for copy in copies:
        copy.wait_recv()
    return (mine[1] + got[1]) + (got[2] + got[3])


def heads_of(x):
    return ((x + 2) % 4, (x + 1) % 4, (x + 3) % 4, x)


def load_weights(wq_hbm, wo_hbm, wv, wo, sem):
    x, _, _, _ = coords()
    copies = []
    for d, head in enumerate(heads_of(x)):
        cols = pl.ds(pl.multiple_of(head * 128, 128), 128)
        for j in range(3):
            copies.append((wq_hbm.at[j, :, cols], wv.at[:, pl.ds(d * 384 + j * 128, 128)]))
        copies.append((wo_hbm.at[cols, :], wo.at[pl.ds(d * 128, 128)]))
    copies = [pltpu.make_async_copy(a, b, sem.at[i]) for i, (a, b) in enumerate(copies)]
    for copy in copies:
        copy.start()
    return copies


NA = 28 * 2 + 5 * 4 * 2 + 4


def project_kernel(
    x_ref, gout_ref, mod_ref, it_ref, wq_hbm, wo_hbm,
    nf, gf, qkvg, inv_ref,
    wv, wo, pq, rq, hq, hqi, oq, iq, pg, rg, hg, hgi, og, ig, mine, got,
    send_sem, recv_sem, load_sem,
):
    x, k, y, z = coords()
    net = Net(send_sem, recv_sem)
    loads = load_weights(wq_hbm, wo_hbm, wv, wo, load_sem)
    enter([CORE, XP, XM, X2, YP, YM, ZP, ZM])
    it = it_ref[0]
    shift, scale, gate = [mod_ref[i, pl.ds(it, 1), :] for i in range(3)]
    gf[y, z] = gout_ref[...]
    cot = Gather(net, gf)
    cot.s1()
    xf = x_ref[...].astype(F32)
    squares = row_sum(net, mine, got, jnp.sum(xf * xf, axis=1, keepdims=True))
    inv = lax.rsqrt(squares / D + EPS)
    inv_ref[...] = inv
    nf[y, z] = (xf * inv[:, :1] * (1.0 + scale) + shift).astype(BF)
    act = Gather(net, nf)
    act.s1()
    for copy in loads:
        copy.wait()
    wo[...] = (wo[...].astype(F32) * gate).astype(BF)
    groups = (act.y, act.ym, act.yp, act.y2)
    rows_q = RowReduce(net, pq, rq, hq, hqi, oq, iq, 384)
    rows_g = RowReduce(net, pg, rg, hg, hgi, og, ig, 128)

    def multiply(s):
        a = nf[groups[s]].reshape(384, 1024)
        for n in range(2):
            cols = pl.ds(n * 768, 768)
            r = jnp.dot(a, wv[:, cols], preferred_element_type=F32)
            pq[s, :, :, cols] = r.astype(BF).reshape(2, HALF, 768)
        rows_q.start(s)

    def multiply_g(s):
        a = gf[groups[s]].reshape(384, 1024)
        r = lax.dot_general(a, wo[...], (((1,), (1,)), ((), ())), preferred_element_type=F32)
        pg[s] = r.astype(BF).reshape(2, HALF, 512)
        rows_g.start(s)

    def finish(s):
        qkvg[groups[s], :, pl.ds(0, 384)] = rows_q.r3(s)

    def finish_g(s):
        qkvg[groups[s], :, pl.ds(384, 128)] = rows_g.r3(s)

    act.s2()
    act.s3()
    multiply(0)
    act.s4()
    cot.s2()
    multiply(1)
    rows_q.r1(0)
    multiply(2)
    rows_q.r1(1)
    rows_q.r2(0)
    act.s5()
    cot.s3()
    multiply(3)
    rows_q.r1(2)
    rows_q.r2(1)
    cot.s4()
    multiply_g(0)
    rows_q.r1(3)
    rows_q.r2(2)
    multiply_g(1)
    multiply_g(2)
    rows_g.r1(0)
    rows_q.r2(3)
    cot.s5()
    multiply_g(3)
    rows_g.r1(1)
    rows_g.r1(2)
    rows_g.r2(0)
    rows_g.r1(3)
    rows_g.r2(1)
    finish(0)
    finish(1)
    rows_g.r2(2)
    rows_g.r2(3)
    finish(2)
    finish(3)
    for s in range(4):
        finish_g(s)
    net.drain()


def attend_kernel(
    qkvg, pos_ref, gp, cx, kv, dk, dv, part, part_in, send_sem, recv_sem
):
    x, k, y, z = coords()
    net = Net(send_sem, recv_sem)
    enter([CORE])
    own = qkvg[...].reshape(768, 512)
    kv[k] = own[:, 128:384]
    exchange = net.send(kv.at[k], kv.at[k], CORE)
    key_pos = jnp.concatenate([pos_ref[pl.ds(0, 1), :], pos_ref[pl.ds(1, 1), :]], axis=1)
    query_pos = jnp.broadcast_to(pos_ref[pl.ds(k, 1), :], (128, 768)).T
    exchange.wait_recv()
    keys = kv[:, :, pl.ds(0, 128)].reshape(1536, 128)
    values = kv[:, :, pl.ds(128, 128)].reshape(1536, 128)
    factor = 1.0 / HEAD_DIM**0.5
    nt = (((1,), (1,)), ((), ()))
    tn = (((0,), (0,)), ((), ()))
    for b in range(4):
        rows = slice(b * 192, b * 192 + 192)
        q, g = own[rows, 0:128], own[rows, 384:512]
        scores = lax.dot_general(q, keys, nt, preferred_element_type=F32) * factor
        scores = jnp.where(key_pos <= query_pos[rows, :1], scores, -1e30)
        weights = jnp.exp(scores - jnp.max(scores, axis=1, keepdims=True))
        probs = weights / jnp.sum(weights, axis=1, keepdims=True)
        probs_b = probs.astype(BF)
        cx[b] = jnp.dot(probs_b, values, preferred_element_type=F32).astype(BF)
        grad_probs = lax.dot_general(g, values, nt, preferred_element_type=F32)
        delta = jnp.sum(probs * grad_probs, axis=1, keepdims=True)
        grad_scores = (probs * (grad_probs - delta) * factor).astype(BF)
        gp[b, :, pl.ds(0, 128)] = jnp.dot(grad_scores, keys, preferred_element_type=F32).astype(BF)
        grad_k = lax.dot_general(grad_scores, q, tn, preferred_element_type=F32)
        grad_v = lax.dot_general(probs_b, g, tn, preferred_element_type=F32)
        if b == 0:
            dk[...] = grad_k.reshape(2, 768, 128)
            dv[...] = grad_v.reshape(2, 768, 128)
        else:
            dk[...] += grad_k.reshape(2, 768, 128)
            dv[...] += grad_v.reshape(2, 768, 128)
    part[:, pl.ds(0, 128)] = dk[1 - k].astype(BF)
    part[:, pl.ds(128, 128)] = dv[1 - k].astype(BF)
    net.send(part, part_in, CORE).wait_recv()
    grad_k = dk[k] + part_in[:, pl.ds(0, 128)].astype(F32)
    grad_v = dv[k] + part_in[:, pl.ds(128, 128)].astype(F32)
    gp[:, :, pl.ds(128, 128)] = grad_k.astype(BF).reshape(4, HALF, 128)
    gp[:, :, pl.ds(256, 128)] = grad_v.astype(BF).reshape(4, HALF, 128)
    net.drain()


class RowGather:
    def __init__(self, net, at, w):
        self.net, self.at, self.w = net, at, w

    def cols(self, d, n=1):
        return pl.ds(d * self.w, n * self.w)

    def start(self):
        own = self.at(slice(None), self.cols(3))
        self.up = self.net.send(own, self.at(slice(None), self.cols(2)), XP)
        self.down = self.net.send(own, self.at(slice(None), self.cols(1)), XM)

    def forward(self):
        lo, hi = pl.ds(0, 96), pl.ds(96, 96)
        self.up.wait_recv()
        self.up2 = self.net.send(self.at(lo, self.cols(2)), self.at(lo, self.cols(0)), XP)
        self.down.wait_recv()
        self.down2 = self.net.send(self.at(hi, self.cols(1)), self.at(hi, self.cols(0)), XM)
        near = self.at(slice(None), self.cols(1, 3))
        self.near = self.net.send(near, near, CORE)

    def finish(self):
        self.up2.wait_recv()
        self.down2.wait_recv()
        far = self.at(slice(None), self.cols(0))
        self.far = self.net.send(far, far, CORE)

    def end(self):
        self.near.wait_recv()
        self.far.wait_recv()


class RingReduce:
    def __init__(self, net, up, down, hop_in, last_in):
        self.net, self.up, self.down, self.hop_in, self.last_in = net, up, down, hop_in, last_in

    def far(self, lo, hi):
        self.a = self.net.send(lo, self.hop_in.at[0], self.up)
        self.b = self.net.send(hi, self.hop_in.at[1], self.down)

    def above(self, lo, whole):
        self.a.wait_recv()
        lo[...] = (lo[...].astype(F32) + self.hop_in[0].astype(F32)).astype(BF)
        self.c = self.net.send(whole, self.last_in.at[0], self.up)

    def below(self, hi, whole):
        self.b.wait_recv()
        hi[...] = (hi[...].astype(F32) + self.hop_in[1].astype(F32)).astype(BF)
        self.d = self.net.send(whole, self.last_in.at[1], self.down)

    def last(self, own):
        own = own.astype(F32)
        self.c.wait_recv()
        self.d.wait_recv()
        return own + self.last_in[0].astype(F32) + self.last_in[1].astype(F32)


NC = 6 * 5 + 28 + 4 + 6


def grads_kernel(
    gp_own, cx_own, nf, gf, x_ref, gout_ref, mod_ref, it_ref, inv_ref, wq_hbm, wo_hbm,
    gin, gmod, gqkv, gow,
    wv, wo, gp, cx, gn, yh0, yi0, t0, zh0, zi0, zh1, zi1, t1, yh1, yi1,
    oq, ow, mine, got, sums, sums_in,
    send_sem, recv_sem, load_sem, store_sem,
):
    x, k, y, z = coords()
    net = Net(send_sem, recv_sem)
    loads = load_weights(wq_hbm, wo_hbm, wv, wo, load_sem)
    enter([CORE, XP, XM, X2, YP, YM, Y2, ZP, ZM, Z2])
    it = it_ref[0]
    shift, scale, gate = [mod_ref[i, pl.ds(it, 1), :] for i in range(3)]
    groups = ((y + 2) % 4, (y + 1) % 4, (y + 3) % 4, y)
    zp, zm, z2 = (z + 1) % 4, (z + 3) % 4, (z + 2) % 4
    gp[:, k, :, pl.ds(3 * 384, 384)] = gp_own[...]
    cx[:, k, :, pl.ds(3 * 128, 128)] = cx_own[...]

    def gather_of(s):
        return RowGather(net, lambda rows, cols: gp.at[groups[s], k, rows, cols], 384)

    def at_context(rows, cols):
        return cx.at[:, k, rows, cols]

    moves = [gather_of(s) for s in range(4)]
    context = RowGather(net, at_context, 128)
    ring_y0 = RingReduce(net, YP, YM, yh0, yi0)
    rings_z1 = [RingReduce(net, ZP, ZM, zh1.at[s], zi1.at[s]) for s in range(4)]
    ring_z0 = RingReduce(net, ZP, ZM, zh0, zi0)
    ring_y1 = RingReduce(net, YP, YM, yh1, yi1)
    lo, hi = pl.ds(0, 48), pl.ds(48, 48)

    def multiply(s):
        a = gp[groups[s]].reshape(384, 1536)
        r = lax.dot_general(a, wv[...], (((1,), (1,)), ((), ())), preferred_element_type=F32)
        gn[s] = r.astype(BF).reshape(4, 96, 1024)

    def z1_far(s):
        rings_z1[s].far(gn.at[s, z2, lo, F1], gn.at[s, z2, hi, F1])

    def z1_near(s):
        rings_z1[s].above(gn.at[s, zp, lo, F1], gn.at[s, zp, :, F1])
        rings_z1[s].below(gn.at[s, zm, hi, F1], gn.at[s, zm, :, F1])

    def z1_last(s):
        return rings_z1[s].last(gn[s, z, :, F1])

    moves[0].start()
    moves[1].start()
    moves[0].forward()
    moves[2].start()
    moves[0].finish()
    moves[1].forward()
    moves[3].start()
    for copy in loads:
        copy.wait()
    moves[0].end()
    multiply(0)
    ring_y0.far(gn.at[0, pl.ds(0, 2), :, F0], gn.at[0, pl.ds(2, 2), :, F0])
    z1_far(0)
    moves[1].finish()
    moves[2].forward()
    context.start()
    moves[1].end()
    multiply(1)
    z1_far(1)
    ring_y0.above(gn.at[1, pl.ds(0, 2), :, F0], gn.at[1, :, :, F0])
    z1_near(0)
    moves[2].finish()
    moves[3].forward()
    moves[2].end()
    multiply(2)
    z1_far(2)
    ring_y0.below(gn.at[2, pl.ds(2, 2), :, F0], gn.at[2, :, :, F0])
    z1_near(1)
    t1[0] = z1_last(0).astype(BF)
    ring_y1.far(t1.at[0, lo], t1.at[0, hi])
    moves[3].finish()
    context.forward()
    moves[3].end()
    multiply(3)
    z1_far(3)
    z1_near(2)
    t1[1] = z1_last(1).astype(BF)
    ring_y1.above(t1.at[1, lo], t1.at[1])
    t0[...] = ring_y0.last(gn[3, :, :, F0]).astype(BF)
    ring_z0.far(t0.at[z2, lo], t0.at[z2, hi])
    z1_near(3)
    t1[2] = z1_last(2).astype(BF)
    ring_y1.below(t1.at[2, hi], t1.at[2])
    context.finish()
    ring_z0.above(t0.at[zp, lo], t0.at[zp])
    ring_z0.below(t0.at[zm, hi], t0.at[zm])

    tn = (((0,), (0,)), ((), ()))
    stores = []

    def store(src, dst):
        copy = pltpu.make_async_copy(src, dst, store_sem.at[len(stores)])
        copy.start()
        stores.append(copy)

    heads = heads_of(x)
    all_gp = gp[...].reshape(1536, 1536)
    for m in range(4):
        rows = pl.ds(m * 256, 256)
        left = nf[:, :, :, rows].reshape(1536, 256)
        oq[rows, :] = lax.dot_general(left, all_gp, tn, preferred_element_type=F32).astype(BF)
    for d, head in enumerate(heads):
        cols = pl.ds(pl.multiple_of(head * 128, 128), 128)
        for j in range(3):
            store(oq.at[:, pl.ds(d * 384 + j * 128, 128)], gqkv.at[j, :, cols])

    context.end()
    all_g = gf[...].reshape(1536, 1024)
    gate_grad = jnp.zeros((1, 1024), F32)
    for m in range(2):
        rows = pl.ds(m * 256, 256)
        left = cx[:, :, :, rows].reshape(1536, 256)
        r = lax.dot_general(left, all_g, tn, preferred_element_type=F32)
        gate_grad += jnp.sum(r * wo[rows, :].astype(F32), axis=0, keepdims=True)
        ow[rows, :] = (r * gate).astype(BF)
    for d, head in enumerate(heads):
        store(ow.at[pl.ds(d * 128, 128)], gow.at[pl.ds(pl.multiple_of(head * 128, 128), 128), :])

    t1[3] = z1_last(3).astype(BF)
    grad0 = ring_z0.last(t0[z])
    grad1 = ring_y1.last(t1[3])
    grad = jnp.concatenate([grad0, grad1], axis=1)
    inv = inv_ref[:, pl.ds(0, 1)]
    x_hat = x_ref[...].astype(F32) * inv
    grad_hat = grad * (1.0 + scale)
    sums[0, pl.ds(0, 1)] = jnp.sum(grad, axis=0, keepdims=True)
    sums[0, pl.ds(1, 1)] = jnp.sum(grad * x_hat, axis=0, keepdims=True)
    sums[0, pl.ds(2, 1)] = gate_grad
    sums[0, pl.ds(3, 5)] = jnp.zeros((5, 1024), F32)
    zc = [net.send(sums.at[0], sums_in.at[i], s) for i, s in enumerate((ZP, ZM, Z2))]
    inner = row_sum(net, mine, got, jnp.sum(grad_hat * x_hat, axis=1, keepdims=True))
    for copy in zc:
        copy.wait_recv()
    sums[1] = (sums[0] + sums_in[0]) + (sums_in[1] + sums_in[2])
    yc = [net.send(sums.at[1], sums_in.at[3 + i], s) for i, s in enumerate((YP, YM, Y2))]
    inner = inner[:, :1] / D
    gin[...] = ((grad_hat - x_hat * inner) * inv + gout_ref[...].astype(F32)).astype(BF)
    for copy in yc:
        copy.wait_recv()
    total = (sums[1] + sums_in[3]) + (sums_in[4] + sums_in[5])
    gmod[...] = total[0:3]
    net.drain()
    for copy in stores:
        copy.wait()


VM = pl.BlockSpec(memory_space=pltpu.VMEM)
SM = pl.BlockSpec(memory_space=pltpu.SMEM)
ANY = pl.BlockSpec(memory_space=pl.ANY)


def sems(n):
    return [pltpu.SemaphoreType.DMA((n,)), pltpu.SemaphoreType.DMA((n,))]


def params(cid):
    return pltpu.CompilerParams(
        collective_id=cid, has_side_effects=True, vmem_limit_bytes=60 << 20
    )


def vb(*shape):
    return pltpu.VMEM(shape, BF)


def vf(*shape):
    return pltpu.VMEM(shape, F32)


def sds(shape, dtype=BF):
    return jax.ShapeDtypeStruct(shape, dtype)


def shards(block_input, modulation, iteration, positions, qkv_weight, out_weight, grad_out):
    mod = modulation.transpose(1, 0, 2)
    wq = qkv_weight.transpose(1, 0, 2)
    pos = positions.astype(F32).reshape(4, 2, HALF).transpose(1, 0, 2).reshape(2, 768)

    def rows(w):
        return [
            vb(4, 2, HALF, 4 * w), vb(4, HALF, 4 * w), vb(4, HALF, w),
            vb(4, 2, 96, w), vb(4, 2, HALF, w), vb(4, 2, HALF, w),
        ]

    nf, gf, qkvg, inv = pl.pallas_call(
        project_kernel,
        name="project",
        out_shape=(sds((4, 4, 96, 1024)), sds((4, 4, 96, 1024)), sds((4, HALF, 512)), sds((96, 128), F32)),
        in_specs=[VM, VM, VM, SM, ANY, ANY],
        out_specs=(VM, VM, VM, VM),
        scratch_shapes=[
            vb(1024, 1536), vb(512, 1024), *rows(384), *rows(128), vf(2, 96, 128), vf(4, 96, 128),
            *sems(NA), pltpu.SemaphoreType.DMA((16,)),
        ],
        compiler_params=params(0),
    )(block_input, grad_out, mod, iteration, wq, out_weight)
    gp, cx = pl.pallas_call(
        attend_kernel,
        name="attend",
        out_shape=(sds((4, HALF, 384)), sds((4, HALF, 128))),
        in_specs=[VM, VM],
        out_specs=(VM, VM),
        scratch_shapes=[
            vb(2, 768, 256), vf(2, 768, 128), vf(2, 768, 128), vb(768, 256), vb(768, 256), *sems(2),
        ],
        compiler_params=params(1),
    )(qkvg, pos)
    gin, gmod, gqkv, gow = pl.pallas_call(
        grads_kernel,
        name="grads",
        out_shape=(sds((96, 1024)), sds((3, 1024), F32), sds((3, 1024, 512)), sds((512, 1024))),
        in_specs=[VM, VM, VM, VM, VM, VM, VM, SM, VM, ANY, ANY],
        out_specs=(VM, VM, ANY, ANY),
        scratch_shapes=[
            vb(1024, 1536), vb(512, 1024), vb(4, 2, HALF, 1536), vb(4, 2, HALF, 512), vb(4, 4, 96, 1024),
            vb(2, 2, 96, 512), vb(2, 4, 96, 512), vb(4, 96, 512), vb(2, 48, 512), vb(2, 96, 512),
            vb(4, 2, 48, 512), vb(4, 2, 96, 512), vb(4, 96, 512), vb(2, 48, 512), vb(2, 96, 512),
            vb(1024, 1536), vb(512, 1024), vf(2, 96, 128), vf(4, 96, 128), vf(2, 8, 1024), vf(6, 8, 1024),
            *sems(NC), pltpu.SemaphoreType.DMA((16,)), pltpu.SemaphoreType.DMA((16,)),
        ],
        compiler_params=params(2),
    )(gp, cx, nf, gf, block_input, grad_out, mod, iteration, inv, wq, out_weight)
    return gin, gqkv.transpose(1, 0, 2), gow, gmod


def solution(mesh):
    placed = (
        P("col", "row"),
        P(None, None, "row"),
        P(),
        P(),
        P("row", None, "col"),
        P("col", "row"),
        P("col", "row"),
    )
    return jax.shard_map(
        shards,
        mesh=mesh,
        in_specs=placed,
        out_specs=(P("col", "row"), P("row", None, "col"), P("col", "row"), P(None, "row")),
        check_vma=False,
    )
```

time: 592 us -> 162 us (0.27)
  waiting for transfers between devices: 356 us -> 0 us
  Pallas kernels: 0 us -> 152 us
  blocking collectives: 100 us -> 0 us
  matrix products: 81.6 us -> 0 us
  local copies, waits for them, and re-layouts: 24.9 us -> 7.81 us
  between operations: 15 us -> 1.31 us
  other arithmetic: 12.2 us -> 0.7 us
    all_gather x6 -> x0, waiting for transfers between devices: 176 us -> none  [the longest x1 42.8 us: shards(): lax.all_gather(normed, 'col', axis=0, tiled=True)]
    pallas_call x0 -> x3, Pallas kernels: none -> 152 us  [the longest x1 75.6 us: shards(): pl.pallas_call(project_kernel, name='project', out_shape=(sds((4, 4, 96,...]
    reduce_scatter x3 -> x0, waiting for transfers between devices: 147 us -> none  [the longest x1 59.8 us: shards(): lax.psum_scatter(contract_cols(panel, w_flat), 'col', scatter_dimension=0...]
    psum x3 -> x0, blocking collectives: 100 us -> none  [the longest x1 72.1 us: shards(): gate_grad = lax.psum(gate_part, 'col')]
    dot_general x11 -> x0, matrix products: 76.2 us -> none  [the longest x2 15.2 us: contract_cols(): lax.dot_general(left, right, (((1,), (1,)), ((), ())), preferred_element_...]
    unnamed x11 -> x0, waiting for transfers between devices: 33 us -> none
    unnamed x24 -> x8, local copies, waits for them, and re-layouts: 17.4 us -> 7.04 us
  transfers between devices with their start and end apart: 10 -> 0, of which waited for: 10 -> 0; matrix products, arithmetic and copies ran while one was open for 13% -> 0% of each run, Pallas kernels for 0% -> 0%
where the time goes in v1:
time: 162 us
  Pallas kernels  152 us (94%)
  local copies, waits for them, and re-layouts  7.81 us (5%)
    pallas_call x1, Pallas kernels, shards(): pl.pallas_call(project_kernel, name='project', out_shape=(sds((4, 4, 96,...  75.6 us
    pallas_call x1, Pallas kernels, shards(): pl.pallas_call(grads_kernel, name='grads', out_shape=(sds((96, 1024)), sd...  63.9 us
    pallas_call x1, Pallas kernels, shards(): pl.pallas_call(attend_kernel, name='attend', out_shape=(sds((4, HALF, 384...  12.6 us
    unnamed x8, local copies, waits for them, and re-layouts  7.04 us

profile of v1, /device:TPU:0, one launch (start us, length us, event | category | flops | bytes accessed | tf_op | source)
XLA Modules:
  0.0 161.9 jit_solution(2730832594597359245)
XLA Ops:
  1.3 0.7 convert_element_type.3
  2.0 0.1 reshape.14
  2.1 0.7 reshape.15.pos_ref
  2.7 75.6 %project.1 = (bf16[4,4,96,1024]{3,2,1,0:T(8,128)(2,1)}, bf16[4,4,96,1024]{3,2,1,0:T(8,128)(2,1)}, bf16[4,192,512]{2,1,0:T(8,128)(2,1)}, f32[96,128]{1,0:T(8,128)}) custom-call(bf16[96,1024]{1,0:T(8,128)(2,1)} %x_ref.3, bf16[96,1024]{1,0:T(8,128)(2,1)} %gout_ref.3, f32[3,8,1024]{2,1,0:T(8,128)} %bitcast.7, s32[1]{0:T(128)S(6)} %copy.16.it_ref, ...), custom_call_target="tpu_custom_call" | custom-call | tf_op jit(solution)/shard_map/project/pallas_call | solution.py:604
  78.4 12.6 %attend.1 = (bf16[4,192,384]{2,1,0:T(8,128)(2,1)}, bf16[4,192,128]{2,1,0:T(8,128)(2,1)}) custom-call(bf16[4,192,512]{2,1,0:T(8,128)(2,1)} %get-tuple-element.14.qkvg, f32[2,768]{1,0:T(2,128)} %reshape.15.pos_ref), custom_call_target="tpu_custom_call" | custom-call | tf_op jit(solution)/shard_map/attend/pallas_call | solution.py:616
  91.0 63.9 %grads.1 = (bf16[96,1024]{1,0:T(8,128)(2,1)}, f32[3,1024]{1,0:T(4,128)}, bf16[3,1024,512]{2,1,0:T(8,128)(2,1)}, bf16[512,1024]{1,0:T(8,128)(2,1)}) custom-call(bf16[4,192,384]{2,1,0:T(8,128)(2,1)} %get-tuple-element.15.gp_own, bf16[4,192,128]{2,1,0:T(8,128)(2,1)} %get-tuple-element.16.cx_own, bf16[4,4,96,1024]{3,2,1,0:T(8,128)(2,1)} %get-tuple-element.17.nf, ...), custom_call_target="tpu_custom_call" | custom-call | tf_op jit(solution)/shard_map/grads/pallas_call | solution.py:627
  154.8 1.6 copy.17
  156.5 0.0 copy-start
  156.5 0.0 copy-start.1
  156.5 3.8 %copy.18 = bf16[1024,3,512]{2,0,1:T(8,128)(2,1)} copy(bf16[1024,3,512]{2,0,1:T(8,128)(2,1)} %bitcast.6) | data formatting | bytes 6291456
  160.3 0.0 copy-done
  160.3 1.0 copy.19
  161.3 0.0 copy-done.1
  161.3 0.6 copy.20
  (1 shorter events, 0.0 us)
Async XLA Ops:
  156.5 3.9 %copy-start = (bf16[512,1024]{1,0:T(8,128)(2,1)S(1)}, bf16[512,1024]{1,0:T(8,128)(2,1)}, u32[]{:S(2)}) copy-start(bf16[512,1024]{1,0:T(8,128)(2,1)} %get-tuple-element.30) | copy-start | bytes 3145732
  156.5 4.8 %copy-start.1 = (f32[3,1024]{1,0:T(4,128)S(1)}, f32[3,1024]{1,0:T(4,128)}, u32[]{:S(2)}) copy-start(f32[3,1024]{1,0:T(4,128)} %get-tuple-element.31) | copy-start | bytes 36868

commit v2 on v1

v2 whole, which is shorter than its diff:
```python
import functools
import jax
import jax.numpy as jnp
from jax import lax
from jax.experimental import pallas as pl
from jax.experimental.pallas import tpu as pltpu
from jax.sharding import PartitionSpec as P

D = 8192
HEAD_DIM = 128
EPS = 1e-06
LOG2E = 1.4426950408889634
MESH = pl.DeviceIdType.MESH
BF = jnp.bfloat16
F32 = jnp.float32

CORE = (0, 1, 0, 0)
XP, XM, X2 = (1, 0, 0, 0), (3, 0, 0, 0), (2, 0, 0, 0)
YP, YM, Y2 = (0, 0, 1, 0), (0, 0, 3, 0), (0, 0, 2, 0)
ZP, ZM, Z2 = (0, 0, 0, 1), (0, 0, 0, 3), (0, 0, 0, 2)

G = 4
HALF = 192
F0, F1 = pl.ds(0, 512), pl.ds(512, 512)


def coords():
    row, col = lax.axis_index("row"), lax.axis_index("col")
    return row // 2, row % 2, col // 4, col % 4


def device(step):
    x, k, y, z = coords()
    dx, dk, dy, dz = step
    x, k, y, z = (x + dx) % 4, (k + dk) % 2, (y + dy) % 4, (z + dz) % 4
    return (x * 2 + k, y * 4 + z)


def enter(steps):
    barrier = pltpu.get_barrier_semaphore()
    for step in steps:
        pl.semaphore_signal(barrier, inc=1, device_id=device(step), device_id_type=MESH)
    pl.semaphore_wait(barrier, len(steps))


class Net:
    def __init__(self, send_sem, recv_sem):
        self.send_sem, self.recv_sem, self.copies = send_sem, recv_sem, []

    def send(self, src, dst, step):
        i = len(self.copies)
        copy = pltpu.make_async_remote_copy(
            src_ref=src,
            dst_ref=dst,
            send_sem=self.send_sem.at[i],
            recv_sem=self.recv_sem.at[i],
            device_id=device(step),
            device_id_type=MESH,
        )
        copy.start()
        self.copies.append(copy)
        return copy

    def drain(self):
        for copy in self.copies:
            copy.wait_send()


class Gather:
    def __init__(self, net, buf):
        _, _, y, z = coords()
        self.net, self.buf, self.y, self.z = net, buf, y, z
        self.yp, self.ym, self.y2 = (y + 1) % 4, (y + 3) % 4, (y + 2) % 4
        self.zp, self.zm, self.z2 = (z + 1) % 4, (z + 3) % 4, (z + 2) % 4
        self.first, self.second = {}, {}

    def put(self, ref, step):
        return self.net.send(ref, ref, step)

    def zsend(self, key, g):
        block = self.buf.at[g, self.z, :, F0]
        self.first[key] = (self.put(block, ZP), self.put(block, ZM))

    def zforward(self, key, g):
        up, down = self.first[key]
        up.wait_recv()
        a = self.put(self.buf.at[g, self.zm, pl.ds(0, 48), F0], ZP)
        down.wait_recv()
        b = self.put(self.buf.at[g, self.zp, pl.ds(48, 48), F0], ZM)
        self.second[key] = (a, b)

    def zend(self, key):
        a, b = self.second[key]
        a.wait_recv()
        b.wait_recv()

    def s1(self):
        f0, f1 = self.buf.at[self.y, self.z, :, F0], self.buf.at[self.y, self.z, :, F1]
        self.a, self.b = self.put(f0, YP), self.put(f0, YM)
        self.c, self.d = self.put(f1, ZP), self.put(f1, ZM)
        self.zsend("own", self.y)

    def s2(self):
        self.c.wait_recv()
        self.c2 = self.put(self.buf.at[self.y, self.zm, pl.ds(0, 48), F1], ZP)
        self.d.wait_recv()
        self.d2 = self.put(self.buf.at[self.y, self.zp, pl.ds(48, 48), F1], ZM)
        self.a.wait_recv()
        self.a2 = self.put(self.buf.at[self.ym, self.z, pl.ds(0, 48), F0], YP)
        self.zsend("ym", self.ym)
        self.b.wait_recv()
        self.b2 = self.put(self.buf.at[self.yp, self.z, pl.ds(48, 48), F0], YM)
        self.zsend("yp", self.yp)

    def s3(self):
        self.c2.wait_recv()
        self.d2.wait_recv()
        group = self.buf.at[self.y, :, :, F1]
        self.gp, self.gm = self.put(group, YP), self.put(group, YM)
        self.zforward("own", self.y)
        self.zend("own")

    def s4a(self):
        self.a2.wait_recv()
        self.b2.wait_recv()
        self.zsend("y2", self.y2)
        self.zforward("ym", self.ym)
        self.zforward("yp", self.yp)

    def s4b(self):
        self.gp.wait_recv()
        self.gp2 = self.put(self.buf.at[self.ym, pl.ds(0, 2), :, F1], YP)
        self.gm.wait_recv()
        self.gm2 = self.put(self.buf.at[self.yp, pl.ds(2, 2), :, F1], YM)

    def s5(self):
        self.zforward("y2", self.y2)
        self.zend("y2")
        self.gp2.wait_recv()
        self.gm2.wait_recv()


class RowReduce:
    def __init__(self, net, own, part, sib, hop, hop_in, out_buf, in_buf, w):
        self.net, self.own, self.part, self.sib = net, own, part, sib
        self.hop, self.hop_in, self.out_buf, self.in_buf, self.w = hop, hop_in, out_buf, in_buf, w
        self.c, self.h, self.f = {}, {}, {}

    def start(self, s):
        self.c[s] = self.net.send(self.part.at[s], self.sib.at[s], CORE)

    def local(self, s, d, rows):
        cols = pl.ds(d * self.w, self.w)
        return self.own[s, rows, cols] + self.sib[s, rows, cols].astype(F32)

    def r1(self, s):
        self.c[s].wait_recv()
        self.hop[s] = self.local(s, 0, pl.ds(0, HALF)).astype(BF)
        self.h[s] = (
            self.net.send(self.hop.at[s, pl.ds(0, 96)], self.hop_in.at[s, 0], XP),
            self.net.send(self.hop.at[s, pl.ds(96, 96)], self.hop_in.at[s, 1], XM),
        )

    def r2(self, s):
        a, b = self.h[s]
        lo, hi = pl.ds(0, 96), pl.ds(96, 96)
        self.out_buf[s, 0, hi] = self.local(s, 1, hi).astype(BF)
        self.out_buf[s, 1, lo] = self.local(s, 2, lo).astype(BF)
        a.wait_recv()
        self.out_buf[s, 0, lo] = (self.local(s, 1, lo) + self.hop_in[s, 0].astype(F32)).astype(BF)
        up = self.net.send(self.out_buf.at[s, 0], self.in_buf.at[s, 0], XP)
        b.wait_recv()
        self.out_buf[s, 1, hi] = (self.local(s, 2, hi) + self.hop_in[s, 1].astype(F32)).astype(BF)
        down = self.net.send(self.out_buf.at[s, 1], self.in_buf.at[s, 1], XM)
        self.f[s] = (up, down)

    def r3(self, s):
        own = self.local(s, 3, pl.ds(0, HALF))
        for copy in self.f[s]:
            copy.wait_recv()
        return (own + self.in_buf[s, 0].astype(F32) + self.in_buf[s, 1].astype(F32)).astype(BF)


OTHERS = [(dx, dk, 0, 0) for dx in range(4) for dk in range(2) if (dx, dk) != (0, 0)]


def row_sum(net, mine, got, value):
    wide = jnp.concatenate([jnp.broadcast_to(value, (96, 128)), jnp.zeros((32, 128), F32)], axis=0)
    mine[...] = wide.T[0:8]
    copies = [net.send(mine, got.at[i], step) for i, step in enumerate(OTHERS)]
    for copy in copies:
        copy.wait_recv()
    total = mine[...]
    for i in range(7):
        total += got[i]
    return jnp.broadcast_to(total[0:1], (128, 128)).T[0:96, 0:1]


def heads_of(x):
    return ((x + 2) % 4, (x + 1) % 4, (x + 3) % 4, x)


def load_weights(wq_hbm, wo_hbm, wv, wo, sem):
    x, _, _, _ = coords()
    copies = []
    for d, head in enumerate(heads_of(x)):
        cols = pl.ds(pl.multiple_of(head * 128, 128), 128)
        for j, place in enumerate((d * 128, 512 + d * 256, 640 + d * 256)):
            copies.append((wq_hbm.at[j, :, cols], wv.at[:, pl.ds(place, 128)]))
        copies.append((wo_hbm.at[cols, :], wo.at[pl.ds(d * 128, 128)]))
    copies = [pltpu.make_async_copy(a, b, sem.at[i]) for i, (a, b) in enumerate(copies)]
    for copy in copies:
        copy.start()
    return copies


class RowGather:
    def __init__(self, net, at, w):
        self.net, self.at, self.w = net, at, w

    def cols(self, d, n=1):
        return pl.ds(d * self.w, n * self.w)

    def start(self):
        own = self.at(slice(None), self.cols(3))
        self.up = self.net.send(own, self.at(slice(None), self.cols(2)), XP)
        self.down = self.net.send(own, self.at(slice(None), self.cols(1)), XM)

    def forward(self):
        lo, hi = pl.ds(0, 96), pl.ds(96, 96)
        self.up.wait_recv()
        self.up2 = self.net.send(self.at(lo, self.cols(2)), self.at(lo, self.cols(0)), XP)
        self.down.wait_recv()
        self.down2 = self.net.send(self.at(hi, self.cols(1)), self.at(hi, self.cols(0)), XM)
        near = self.at(slice(None), self.cols(1, 3))
        self.near = self.net.send(near, near, CORE)

    def finish(self):
        self.up2.wait_recv()
        self.down2.wait_recv()
        far = self.at(slice(None), self.cols(0))
        self.far = self.net.send(far, far, CORE)

    def end(self):
        self.near.wait_recv()
        self.far.wait_recv()


class RingReduce:
    def __init__(self, net, up, down, hop_in, last_in):
        self.net, self.up, self.down, self.hop_in, self.last_in = net, up, down, hop_in, last_in

    def far(self, lo, hi):
        self.a = self.net.send(lo, self.hop_in.at[0], self.up)
        self.b = self.net.send(hi, self.hop_in.at[1], self.down)

    def above(self, lo, whole):
        self.a.wait_recv()
        lo[...] = (lo[...].astype(F32) + self.hop_in[0].astype(F32)).astype(BF)
        self.c = self.net.send(whole, self.last_in.at[0], self.up)

    def below(self, hi, whole):
        self.b.wait_recv()
        hi[...] = (hi[...].astype(F32) + self.hop_in[1].astype(F32)).astype(BF)
        self.d = self.net.send(whole, self.last_in.at[1], self.down)

    def last(self, own):
        own = own.astype(F32)
        self.c.wait_recv()
        self.d.wait_recv()
        return own + self.last_in[0].astype(F32) + self.last_in[1].astype(F32)


NT = (((1,), (1,)), ((), ()))
TN = (((0,), (0,)), ((), ()))
N_COPIES = 28 * 2 + 5 * 4 * 2 + 14 + 4 + 6 * 9 + 1 + 28 + 6


def kernel(
    x_ref, gout_ref, mod_ref, it_ref, pos_ref, wq_hbm, wo_hbm,
    gin, gmod, gqkv, gow,
    nf, gf, qkvg, wv, wo, wog,
    aq, pq, rq, hq, hqi, oq, iq, ag, pg, rg, hg, hgi, og, ig, mine, got, mine2, got2,
    kv, wts, pos_t, stats, dk, dv, part, part_in,
    gpq, gpkv, cx, gnq, gn, yh0, yi0, t0, zh0, zi0, zh1, zi1, t1, yh1, yi1,
    outq, ow, sums, sums_z, sums_y,
    send_sem, recv_sem, load_sem, store_sem,
):
    x, k, y, z = coords()
    net = Net(send_sem, recv_sem)
    loads = load_weights(wq_hbm, wo_hbm, wv, wo, load_sem)
    enter(OTHERS + [YP, YM, Y2, ZP, ZM, Z2])
    it = it_ref[0]
    shift, scale, gate = [mod_ref[i, pl.ds(it, 1), :] for i in range(3)]

    gf[y, z] = gout_ref[...]
    cot = Gather(net, gf)
    cot.s1()
    xf = x_ref[...].astype(F32)
    squares = row_sum(net, mine, got, jnp.sum(xf * xf, axis=1, keepdims=True))
    inv = lax.rsqrt(squares / D + EPS)
    nf[y, z] = (xf * inv * (1.0 + scale) + shift).astype(BF)
    act = Gather(net, nf)
    act.s1()
    for copy in loads:
        copy.wait()
    wog[...] = (wo[...].astype(F32) * gate).astype(BF)
    key_pos = jnp.concatenate([pos_ref[pl.ds(0, 1), :], pos_ref[pl.ds(1, 1), :]], axis=1)
    pos_t[...] = jnp.broadcast_to(pos_ref[pl.ds(k, 1), :], (128, 768)).T.reshape(4, HALF, 128)
    order = (act.y, act.ym, act.yp, act.y2)
    rows_q = RowReduce(net, aq, pq, rq, hq, hqi, oq, iq, 384)
    rows_g = RowReduce(net, ag, pg, rg, hg, hgi, og, ig, 128)

    def half_of(buf, s, h):
        return buf[order[s], pl.ds(2 * h, 2)].reshape(HALF, 1024)

    def multiply(s):
        for h, dst in ((1 - k, pq), (k, aq)):
            a = half_of(nf, s, h)
            r = jnp.dot(a, wv[:, pl.ds(0, 512)], preferred_element_type=F32).astype(dst.dtype)
            for d in range(4):
                dst[s, :, pl.ds(d * 384, 128)] = r[:, d * 128 : d * 128 + 128]
            r = jnp.dot(a, wv[:, pl.ds(512, 1024)], preferred_element_type=F32).astype(dst.dtype)
            for d in range(4):
                dst[s, :, pl.ds(d * 384 + 128, 256)] = r[:, d * 256 : d * 256 + 256]
            if dst is pq:
                rows_q.start(s)

    def multiply_g(s):
        for h, dst in ((1 - k, pg), (k, ag)):
            r = lax.dot_general(half_of(gf, s, h), wog[...], NT, preferred_element_type=F32)
            dst[s] = r.astype(dst.dtype)
            if dst is pg:
                rows_g.start(s)

    swaps = []

    def finish(s):
        r = rows_q.r3(s)
        qkvg[order[s], :, pl.ds(0, 128)] = r[:, 0:128]
        kv[k, order[s]] = r[:, 128:384]
        half = kv.at[k, order[s]]
        swaps.append(net.send(half, half, CORE))

    def finish_g(s):
        qkvg[order[s], :, pl.ds(128, 128)] = rows_g.r3(s)

    act.s2()
    act.s3()
    multiply(0)
    act.s4a()
    rows_q.r1(0)
    act.s4b()
    cot.s2()
    act.zend("ym")
    multiply(1)
    rows_q.r2(0)
    act.zend("yp")
    multiply(2)
    rows_q.r1(1)
    act.s5()
    cot.s3()
    multiply(3)
    rows_q.r1(2)
    rows_q.r2(1)
    finish(0)
    cot.s4a()
    rows_q.r1(3)
    rows_q.r2(2)
    cot.s4b()
    finish(1)
    multiply_g(0)
    rows_q.r2(3)
    cot.zend("ym")
    multiply_g(1)
    rows_g.r1(0)
    finish(2)
    cot.zend("yp")
    multiply_g(2)
    rows_g.r1(1)
    finish(3)
    cot.s5()
    multiply_g(3)
    rows_g.r1(2)
    rows_g.r2(0)
    rows_g.r2(1)

    groups = ((y + 2) % 4, (y + 1) % 4, (y + 3) % 4, y)
    for copy in swaps:
        copy.wait_recv()
    keys = kv[:, :, :, pl.ds(0, 128)].reshape(1536, 128)
    values = kv[:, :, :, pl.ds(128, 128)].reshape(1536, 128)
    factor = 1.0 / HEAD_DIM**0.5

    def attend(s):
        q = qkvg[groups[s], :, pl.ds(0, 128)]
        scores = lax.dot_general(q, keys, NT, preferred_element_type=F32)
        scores = jnp.where(key_pos <= pos_t[groups[s], :, pl.ds(0, 1)], scores, -1e30)
        peak = jnp.max(scores, axis=1, keepdims=True)
        weights = jnp.exp2((scores - peak) * (factor * LOG2E))
        wts[s] = weights
        inverse = 1.0 / jnp.sum(weights, axis=1, keepdims=True)
        stats[s] = jnp.broadcast_to(inverse, (HALF, 128))
        probs_b = (weights * inverse).astype(BF)
        r = jnp.dot(probs_b, values, preferred_element_type=F32)
        cx[groups[s], k, :, pl.ds(384, 128)] = r.astype(BF)

    def attend_grad(s):
        q = qkvg[groups[s], :, pl.ds(0, 128)]
        g = qkvg[groups[s], :, pl.ds(128, 128)]
        weights, inverse = wts[s], stats[s, :, pl.ds(0, 1)]
        probs_b = (weights * inverse).astype(BF)
        grad_probs = lax.dot_general(g, values, NT, preferred_element_type=F32)
        delta = jnp.sum(weights * grad_probs, axis=1, keepdims=True) * inverse
        grad_scores = (weights * (grad_probs - delta) * (inverse * factor)).astype(BF)
        r = jnp.dot(grad_scores, keys, preferred_element_type=F32)
        gpq[groups[s], k, :, pl.ds(384, 128)] = r.astype(BF)
        grad_k = lax.dot_general(grad_scores, q, TN, preferred_element_type=F32)
        grad_v = lax.dot_general(probs_b, g, TN, preferred_element_type=F32)
        if s == 0:
            dk[...] = grad_k.reshape(2, 768, 128)
            dv[...] = grad_v.reshape(2, 768, 128)
        else:
            dk[...] += grad_k.reshape(2, 768, 128)
            dv[...] += grad_v.reshape(2, 768, 128)

    def gather_q(s):
        return RowGather(net, lambda rows, cols: gpq.at[groups[s], k, rows, cols], 128)

    def gather_kv(s):
        return RowGather(net, lambda rows, cols: gpkv.at[groups[s], k, rows, cols], 256)

    moves_q = [gather_q(s) for s in range(4)]
    moves_kv = [gather_kv(s) for s in range(4)]
    context = RowGather(net, lambda rows, cols: cx.at[:, k, rows, cols], 128)

    attend(0)
    rows_g.r1(3)
    rows_g.r2(2)
    finish_g(0)
    finish_g(1)
    attend(1)
    rows_g.r2(3)
    finish_g(2)
    attend(2)
    attend(3)
    context.start()
    finish_g(3)
    attend_grad(0)
    moves_q[0].start()
    context.forward()
    attend_grad(1)
    moves_q[1].start()
    moves_q[0].forward()
    context.finish()
    attend_grad(2)
    moves_q[2].start()
    moves_q[1].forward()
    moves_q[0].finish()
    attend_grad(3)
    part[:, pl.ds(0, 128)] = dk[1 - k].astype(BF)
    part[:, pl.ds(128, 128)] = dv[1 - k].astype(BF)
    swap = net.send(part, part_in, CORE)
    moves_q[3].start()
    moves_q[2].forward()
    moves_q[1].finish()

    stores = []

    def store(src, dst):
        copy = pltpu.make_async_copy(src, dst, store_sem.at[len(stores)])
        copy.start()
        stores.append(copy)

    heads = heads_of(x)
    head_at = [pl.ds(pl.multiple_of(head * 128, 128), 128) for head in heads]
    ring_y0 = RingReduce(net, YP, YM, yh0, yi0)
    rings_z1 = [RingReduce(net, ZP, ZM, zh1.at[s], zi1.at[s]) for s in range(4)]
    ring_z0 = RingReduce(net, ZP, ZM, zh0, zi0)
    ring_y1 = RingReduce(net, YP, YM, yh1, yi1)
    lo, hi = pl.ds(0, 48), pl.ds(48, 48)
    zp, zm, z2 = (z + 1) % 4, (z + 3) % 4, (z + 2) % 4

    def normed_q(s):
        moves_q[s].end()
        a = gpq[groups[s]].reshape(384, 512)
        gnq[s] = lax.dot_general(a, wv[:, pl.ds(0, 512)], NT, preferred_element_type=F32)

    def normed_kv(s):
        moves_kv[s].end()
        a = gpkv[groups[s]].reshape(384, 1024)
        r = lax.dot_general(a, wv[:, pl.ds(512, 1024)], NT, preferred_element_type=F32)
        gn[s] = (gnq[s] + r).astype(BF).reshape(4, 96, 1024)

    def out_weight():
        context.end()
        all_g = gf[...].reshape(1536, 1024)
        gate_grad = jnp.zeros((1, 1024), F32)
        for m in range(2):
            rows = pl.ds(m * 256, 256)
            left = cx[:, :, :, rows].reshape(1536, 256)
            r = lax.dot_general(left, all_g, TN, preferred_element_type=F32)
            gate_grad += jnp.sum(r * wo[rows, :].astype(F32), axis=0, keepdims=True)
            ow[rows, :] = (r * gate).astype(BF)
        for d in range(4):
            store(ow.at[pl.ds(d * 128, 128)], gow.at[head_at[d], :])
        return gate_grad

    def weight_q(m):
        rows = pl.ds(m * 256, 256)
        left = nf[:, :, :, rows].reshape(1536, 256)
        right = gpq[...].reshape(1536, 512)
        r = lax.dot_general(left, right, TN, preferred_element_type=F32)
        outq[rows, pl.ds(0, 512)] = r.astype(BF)

    def weight_kv(m):
        rows = pl.ds(m * 256, 256)
        left = nf[:, :, :, rows].reshape(1536, 256)
        right = gpkv[...].reshape(1536, 1024)
        r = lax.dot_general(left, right, TN, preferred_element_type=F32)
        outq[rows, pl.ds(512, 1024)] = r.astype(BF)

    def z1_far(s):
        rings_z1[s].far(gn.at[s, z2, lo, F1], gn.at[s, z2, hi, F1])

    def z1_near(s):
        rings_z1[s].above(gn.at[s, zp, lo, F1], gn.at[s, zp, :, F1])
        rings_z1[s].below(gn.at[s, zm, hi, F1], gn.at[s, zm, :, F1])

    def z1_last(s):
        return rings_z1[s].last(gn[s, z, :, F1])

    swap.wait_recv()
    for cols, total in ((pl.ds(0, 128), dk), (pl.ds(128, 128), dv)):
        r = (total[k] + part_in[:, cols].astype(F32)).astype(BF)
        gpkv[:, k, :, pl.ds(3 * 256 + cols.start, 128)] = r.reshape(4, HALF, 128)
    moves_kv[0].start()
    moves_q[3].forward()
    moves_q[2].finish()
    moves_kv[1].start()
    normed_q(0)
    moves_kv[0].forward()
    moves_q[3].finish()
    moves_kv[2].start()
    normed_q(1)
    normed_q(2)
    moves_kv[1].forward()
    moves_kv[0].finish()
    moves_kv[3].start()
    normed_q(3)
    gate_grad = out_weight()
    normed_kv(0)
    ring_y0.far(gn.at[0, pl.ds(0, 2), :, F0], gn.at[0, pl.ds(2, 2), :, F0])
    z1_far(0)
    moves_kv[2].forward()
    moves_kv[1].finish()
    normed_kv(1)
    z1_far(1)
    ring_y0.above(gn.at[1, pl.ds(0, 2), :, F0], gn.at[1, :, :, F0])
    z1_near(0)
    moves_kv[3].forward()
    moves_kv[2].finish()
    normed_kv(2)
    z1_far(2)
    ring_y0.below(gn.at[2, pl.ds(2, 2), :, F0], gn.at[2, :, :, F0])
    z1_near(1)
    t1[0] = z1_last(0).astype(BF)
    ring_y1.far(t1.at[0, lo], t1.at[0, hi])
    moves_kv[3].finish()
    weight_q(0)
    weight_q(1)
    normed_kv(3)
    z1_far(3)
    z1_near(2)
    t1[1] = z1_last(1).astype(BF)
    ring_y1.above(t1.at[1, lo], t1.at[1])
    t0[...] = ring_y0.last(gn[3, :, :, F0]).astype(BF)
    ring_z0.far(t0.at[z2, lo], t0.at[z2, hi])
    z1_near(3)
    t1[2] = z1_last(2).astype(BF)
    ring_y1.below(t1.at[2, hi], t1.at[2])
    weight_q(2)
    ring_z0.above(t0.at[zp, lo], t0.at[zp])
    ring_z0.below(t0.at[zm, hi], t0.at[zm])
    weight_q(3)
    t1[3] = z1_last(3).astype(BF)
    weight_kv(0)

    grad0 = ring_z0.last(t0[z])
    grad1 = ring_y1.last(t1[3])
    grad = jnp.concatenate([grad0, grad1], axis=1)
    x_hat = x_ref[...].astype(F32) * inv
    grad_hat = grad * (1.0 + scale)
    sums[0, pl.ds(0, 1)] = jnp.sum(grad, axis=0, keepdims=True)
    sums[0, pl.ds(1, 1)] = jnp.sum(grad * x_hat, axis=0, keepdims=True)
    sums[0, pl.ds(2, 1)] = gate_grad
    sums[0, pl.ds(3, 5)] = jnp.zeros((5, 1024), F32)
    sums_z[z] = sums[0]
    zc = [net.send(sums.at[0], sums_z.at[z], step) for step in (ZP, ZM, Z2)]
    inner = row_sum(net, mine2, got2, jnp.sum(grad_hat * x_hat, axis=1, keepdims=True)) / D
    for copy in zc:
        copy.wait_recv()
    sums[1] = (sums_z[0] + sums_z[1]) + (sums_z[2] + sums_z[3])
    sums_y[y] = sums[1]
    yc = [net.send(sums.at[1], sums_y.at[y], step) for step in (YP, YM, Y2)]
    gin[...] = ((grad_hat - x_hat * inner) * inv + gout_ref[...].astype(F32)).astype(BF)
    for m in range(1, 4):
        weight_kv(m)
    for d in range(4):
        for j, place in enumerate((d * 128, 512 + d * 256, 640 + d * 256)):
            store(outq.at[:, pl.ds(place, 128)], gqkv.at[j, :, head_at[d]])
    for copy in yc:
        copy.wait_recv()
    gmod[...] = ((sums_y[0] + sums_y[1]) + (sums_y[2] + sums_y[3]))[0:3]
    net.drain()
    for copy in stores:
        copy.wait()


VM = pl.BlockSpec(memory_space=pltpu.VMEM)
SM = pl.BlockSpec(memory_space=pltpu.SMEM)
ANY = pl.BlockSpec(memory_space=pl.ANY)


def vb(*shape):
    return pltpu.VMEM(shape, BF)


def vf(*shape):
    return pltpu.VMEM(shape, F32)


def sds(shape, dtype=BF):
    return jax.ShapeDtypeStruct(shape, dtype)


def shards(block_input, modulation, iteration, positions, qkv_weight, out_weight, grad_out):
    mod = modulation.transpose(1, 0, 2)
    wq = qkv_weight.transpose(1, 0, 2)
    pos = positions.astype(F32).reshape(4, 2, HALF).transpose(1, 0, 2).reshape(2, 768)

    def rows(w):
        return [
            vf(4, HALF, 4 * w), vb(4, HALF, 4 * w), vb(4, HALF, 4 * w), vb(4, HALF, w),
            vb(4, 2, 96, w), vb(4, 2, HALF, w), vb(4, 2, HALF, w),
        ]

    gin, gmod, gqkv, gow = pl.pallas_call(
        kernel,
        name="block_backward",
        out_shape=(sds((96, 1024)), sds((3, 1024), F32), sds((3, 1024, 512)), sds((512, 1024))),
        in_specs=[VM, VM, VM, SM, VM, ANY, ANY],
        out_specs=(VM, VM, ANY, ANY),
        scratch_shapes=[
            vb(4, 4, 96, 1024), vb(4, 4, 96, 1024), vb(4, HALF, 256),
            vb(1024, 1536), vb(512, 1024), vb(512, 1024),
            *rows(384), *rows(128), vf(8, 128), vf(7, 8, 128), vf(8, 128), vf(7, 8, 128),
            vb(2, 4, HALF, 256), vf(4, HALF, 1536), vf(4, HALF, 128), vf(4, HALF, 128),
            vf(2, 768, 128), vf(2, 768, 128), vb(768, 256), vb(768, 256),
            vb(4, 2, HALF, 512), vb(4, 2, HALF, 1024), vb(4, 2, HALF, 512),
            vf(4, 384, 1024), vb(4, 4, 96, 1024),
            vb(2, 2, 96, 512), vb(2, 4, 96, 512), vb(4, 96, 512), vb(2, 48, 512), vb(2, 96, 512),
            vb(4, 2, 48, 512), vb(4, 2, 96, 512), vb(4, 96, 512), vb(2, 48, 512), vb(2, 96, 512),
            vb(1024, 1536), vb(512, 1024), vf(2, 8, 1024), vf(4, 8, 1024), vf(4, 8, 1024),
            pltpu.SemaphoreType.DMA((N_COPIES,)), pltpu.SemaphoreType.DMA((N_COPIES,)),
            pltpu.SemaphoreType.DMA((16,)), pltpu.SemaphoreType.DMA((16,)),
        ],
        compiler_params=pltpu.CompilerParams(
            collective_id=0, has_side_effects=True, vmem_limit_bytes=63 << 20
        ),
    )(block_input, grad_out, mod, iteration, pos, wq, out_weight)
    return gin, gqkv.transpose(1, 0, 2), gow, gmod


def solution(mesh):
    placed = (
        P("col", "row"),
        P(None, None, "row"),
        P(),
        P(),
        P("row", None, "col"),
        P("col", "row"),
        P("col", "row"),
    )
    return jax.shard_map(
        shards,
        mesh=mesh,
        in_specs=placed,
        out_specs=(P("col", "row"), P("row", None, "col"), P("col", "row"), P(None, "row")),
        check_vma=False,
    )
```

time: 162 us -> 152 us (0.938)
  Pallas kernels: 152 us -> 141 us
    pallas_call x3 -> x1, Pallas kernels: 152 us -> 141 us  [shards(): pl.pallas_call(kernel, name='block_backward', out_shape=(sds((96, 1024)),...]
where the time goes in v2:
time: 152 us; the launch traced here: 151 us
  Pallas kernels  141 us (93%)
  local copies, waits for them, and re-layouts  7.81 us (5%)
    pallas_call x1, Pallas kernels, shards(): pl.pallas_call(kernel, name='block_backward', out_shape=(sds((96, 1024)),...  141 us
    unnamed x8, local copies, waits for them, and re-layouts  7.04 us

profile of v2, /device:TPU:0, one launch (start us, length us, event | category | flops | bytes accessed | tf_op | source)
XLA Modules:
  0.0 151.2 jit_solution(9068168547429069123)
XLA Ops:
  1.3 0.7 convert_element_type.3
  2.0 0.1 reshape.14
  2.1 0.7 reshape.15.pos_ref
  2.7 141.3 %block_backward.1 = (bf16[96,1024]{1,0:T(8,128)(2,1)}, f32[3,1024]{1,0:T(4,128)}, bf16[3,1024,512]{2,1,0:T(8,128)(2,1)}, bf16[512,1024]{1,0:T(8,128)(2,1)}) custom-call(bf16[96,1024]{1,0:T(8,128)(2,1)} %x_ref.1, bf16[96,1024]{1,0:T(8,128)(2,1)} %gout_ref.1, f32[3,8,1024]{2,1,0:T(8,128)} %bitcast.6, s32[1]{0:T(128)S(6)} %copy.16.it_ref, ...), custom_call_target="tpu_custom_call" | custom-call | tf_op jit(solution)/shard_map/block_backward/pallas_call | solution.py:648
  144.1 1.6 %copy.17 = bf16[96,1024]{1,0:T(8,128)(2,1)} copy(bf16[96,1024]{1,0:T(8,128)(2,1)} %get-tuple-element.16) | data formatting | bytes 393216
  145.7 0.0 copy-start
  145.7 0.0 copy-start.1
  145.7 3.8 %copy.18 = bf16[1024,3,512]{2,0,1:T(8,128)(2,1)} copy(bf16[1024,3,512]{2,0,1:T(8,128)(2,1)} %bitcast.4) | data formatting | bytes 6291456
  149.6 0.0 copy-done
  149.6 1.0 copy.19
  150.5 0.0 copy-done.1
  150.5 0.6 copy.20
  (1 shorter events, 0.0 us)
Async XLA Ops:
  145.7 3.9 %copy-start = (bf16[512,1024]{1,0:T(8,128)(2,1)S(1)}, bf16[512,1024]{1,0:T(8,128)(2,1)}, u32[]{:S(2)}) copy-start(bf16[512,1024]{1,0:T(8,128)(2,1)} %get-tuple-element.18) | copy-start | bytes 3145732
  145.7 4.8 %copy-start.1 = (f32[3,1024]{1,0:T(4,128)S(1)}, f32[3,1024]{1,0:T(4,128)}, u32[]{:S(2)}) copy-start(f32[3,1024]{1,0:T(4,128)} %get-tuple-element.19) | copy-start | bytes 36868

commit v3 on v2

--- a/solution.py
+++ b/solution.py
@@ -66,78 +66,87 @@
             copy.wait_send()
 
 
+class Line:
+    def __init__(self, net, at, up, down, rows):
+        self.net, self.at, self.up, self.down, self.half = net, at, up, down, rows // 2
+        self.all = pl.ds(0, rows)
+
+    def put(self, step, rows, way):
+        ref = self.at(step, rows)
+        return self.net.send(ref, ref, way)
+
+    def start(self):
+        self.a, self.b = self.put(0, self.all, self.up), self.put(0, self.all, self.down)
+
+    def forward_up(self):
+        self.a.wait_recv()
+        self.c = self.put(3, pl.ds(0, self.half), self.up)
+
+    def forward_down(self):
+        self.b.wait_recv()
+        self.d = self.put(1, pl.ds(self.half, self.half), self.down)
+
+    def forward(self):
+        self.forward_up()
+        self.forward_down()
+
+    def end(self):
+        self.c.wait_recv()
+        self.d.wait_recv()
+
+
 class Gather:
     def __init__(self, net, buf):
         _, _, y, z = coords()
-        self.net, self.buf, self.y, self.z = net, buf, y, z
-        self.yp, self.ym, self.y2 = (y + 1) % 4, (y + 3) % 4, (y + 2) % 4
-        self.zp, self.zm, self.z2 = (z + 1) % 4, (z + 3) % 4, (z + 2) % 4
-        self.first, self.second = {}, {}
-
-    def put(self, ref, step):
-        return self.net.send(ref, ref, step)
-
-    def zsend(self, key, g):
-        block = self.buf.at[g, self.z, :, F0]
-        self.first[key] = (self.put(block, ZP), self.put(block, ZM))
-
-    def zforward(self, key, g):
-        up, down = self.first[key]
-        up.wait_recv()
-        a = self.put(self.buf.at[g, self.zm, pl.ds(0, 48), F0], ZP)
-        down.wait_recv()
-        b = self.put(self.buf.at[g, self.zp, pl.ds(48, 48), F0], ZM)
-        self.second[key] = (a, b)
-
-    def zend(self, key):
-        a, b = self.second[key]
-        a.wait_recv()
-        b.wait_recv()
+
+        def along_y(zz, cols):
+            return Line(net, lambda n, rows: buf.at[(y + n) % 4, zz, rows, cols], YP, YM, 96)
+
+        def along_z(yy, cols):
+            return Line(net, lambda n, rows: buf.at[yy, (z + n) % 4, rows, cols], ZP, ZM, 96)
+
+        self.a, self.b = along_y(z, F0), along_z(y, F1)
+        self.zs = [along_z((y + n) % 4, F0) for n in range(4)]
+        self.ys = [along_y((z + n) % 4, F1) for n in range(4)]
 
     def s1(self):
-        f0, f1 = self.buf.at[self.y, self.z, :, F0], self.buf.at[self.y, self.z, :, F1]
-        self.a, self.b = self.put(f0, YP), self.put(f0, YM)
-        self.c, self.d = self.put(f1, ZP), self.put(f1, ZM)
-        self.zsend("own", self.y)
+        for line in (self.a, self.b, self.zs[0], self.ys[0]):
+            line.start()
 
     def s2(self):
-        self.c.wait_recv()
-        self.c2 = self.put(self.buf.at[self.y, self.zm, pl.ds(0, 48), F1], ZP)
-        self.d.wait_recv()
-        self.d2 = self.put(self.buf.at[self.y, self.zp, pl.ds(48, 48), F1], ZM)
-        self.a.wait_recv()
-        self.a2 = self.put(self.buf.at[self.ym, self.z, pl.ds(0, 48), F0], YP)
-        self.zsend("ym", self.ym)
-        self.b.wait_recv()
-        self.b2 = self.put(self.buf.at[self.yp, self.z, pl.ds(48, 48), F0], YM)
-        self.zsend("yp", self.yp)
+        self.a.forward_up()
+        self.zs[3].start()
+        self.b.forward_up()
+        self.ys[3].start()
+        self.a.forward_down()
+        self.zs[1].start()
+        self.b.forward_down()
+        self.ys[1].start()
 
     def s3(self):
-        self.c2.wait_recv()
-        self.d2.wait_recv()
-        group = self.buf.at[self.y, :, :, F1]
-        self.gp, self.gm = self.put(group, YP), self.put(group, YM)
-        self.zforward("own", self.y)
-        self.zend("own")
-
-    def s4a(self):
-        self.a2.wait_recv()
-        self.b2.wait_recv()
-        self.zsend("y2", self.y2)
-        self.zforward("ym", self.ym)
-        self.zforward("yp", self.yp)
-
-    def s4b(self):
-        self.gp.wait_recv()
-        self.gp2 = self.put(self.buf.at[self.ym, pl.ds(0, 2), :, F1], YP)
-        self.gm.wait_recv()
-        self.gm2 = self.put(self.buf.at[self.yp, pl.ds(2, 2), :, F1], YM)
+        self.zs[0].forward()
+        self.ys[0].forward()
+        self.a.end()
+        self.zs[2].start()
+        self.b.end()
+        self.ys[2].start()
+        self.zs[0].end()
+
+    def s4(self):
+        for n in (3, 1):
+            self.zs[n].forward()
+            self.ys[n].forward()
 
     def s5(self):
-        self.zforward("y2", self.y2)
-        self.zend("y2")
-        self.gp2.wait_recv()
-        self.gm2.wait_recv()
+        self.zs[2].forward()
+        self.ys[2].forward()
+        self.zs[3].end()
+        self.zs[1].end()
+
+    def s6(self):
+        self.zs[2].end()
+        for line in self.ys:
+            line.end()
 
 
 class RowReduce:
@@ -153,26 +162,32 @@
         cols = pl.ds(d * self.w, self.w)
         return self.own[s, rows, cols] + self.sib[s, rows, cols].astype(F32)
 
+    def put(self, s, i, rows, way):
+        copy = self.net.send(self.out_buf.at[s, i, rows], self.in_buf.at[s, i, rows], way)
+        self.f.setdefault(s, []).append(copy)
+
     def r1(self, s):
+        lo, hi = pl.ds(0, 96), pl.ds(96, 96)
         self.c[s].wait_recv()
         self.hop[s] = self.local(s, 0, pl.ds(0, HALF)).astype(BF)
         self.h[s] = (
-            self.net.send(self.hop.at[s, pl.ds(0, 96)], self.hop_in.at[s, 0], XP),
-            self.net.send(self.hop.at[s, pl.ds(96, 96)], self.hop_in.at[s, 1], XM),
+            self.net.send(self.hop.at[s, lo], self.hop_in.at[s, 0], XP),
+            self.net.send(self.hop.at[s, hi], self.hop_in.at[s, 1], XM),
         )
+        self.out_buf[s, 0, hi] = self.local(s, 1, hi).astype(BF)
+        self.put(s, 0, hi, XP)
+        self.out_buf[s, 1, lo] = self.local(s, 2, lo).astype(BF)
+        self.put(s, 1, lo, XM)
 
     def r2(self, s):
         a, b = self.h[s]
         lo, hi = pl.ds(0, 96), pl.ds(96, 96)
-        self.out_buf[s, 0, hi] = self.local(s, 1, hi).astype(BF)
-        self.out_buf[s, 1, lo] = self.local(s, 2, lo).astype(BF)
         a.wait_recv()
         self.out_buf[s, 0, lo] = (self.local(s, 1, lo) + self.hop_in[s, 0].astype(F32)).astype(BF)
-        up = self.net.send(self.out_buf.at[s, 0], self.in_buf.at[s, 0], XP)
+        self.put(s, 0, lo, XP)
         b.wait_recv()
         self.out_buf[s, 1, hi] = (self.local(s, 2, hi) + self.hop_in[s, 1].astype(F32)).astype(BF)
-        down = self.net.send(self.out_buf.at[s, 1], self.in_buf.at[s, 1], XM)
-        self.f[s] = (up, down)
+        self.put(s, 1, hi, XM)
 
     def r3(self, s):
         own = self.local(s, 3, pl.ds(0, HALF))
@@ -184,16 +199,20 @@
 OTHERS = [(dx, dk, 0, 0) for dx in range(4) for dk in range(2) if (dx, dk) != (0, 0)]
 
 
-def row_sum(net, mine, got, value):
-    wide = jnp.concatenate([jnp.broadcast_to(value, (96, 128)), jnp.zeros((32, 128), F32)], axis=0)
-    mine[...] = wide.T[0:8]
-    copies = [net.send(mine, got.at[i], step) for i, step in enumerate(OTHERS)]
-    for copy in copies:
-        copy.wait_recv()
-    total = mine[...]
-    for i in range(7):
-        total += got[i]
-    return jnp.broadcast_to(total[0:1], (128, 128)).T[0:96, 0:1]
+class RowSum:
+    def __init__(self, net, mine, got, value):
+        self.mine, self.got = mine, got
+        wide = jnp.concatenate([jnp.broadcast_to(value, (96, 128)), jnp.zeros((32, 128), F32)], axis=0)
+        mine[...] = wide.T[0:8]
+        self.copies = [net.send(mine, got.at[i], step) for i, step in enumerate(OTHERS)]
+
+    def total(self):
+        for copy in self.copies:
+            copy.wait_recv()
+        total = self.mine[...]
+        for i in range(7):
+            total += self.got[i]
+        return jnp.broadcast_to(total[0:1], (128, 128)).T[0:96, 0:1]
 
 
 def heads_of(x):
@@ -247,33 +266,45 @@
 
 
 class RingReduce:
-    def __init__(self, net, up, down, hop_in, last_in):
+    def __init__(self, net, up, down, hop_in, last_in, lo, hi):
         self.net, self.up, self.down, self.hop_in, self.last_in = net, up, down, hop_in, last_in
-
-    def far(self, lo, hi):
-        self.a = self.net.send(lo, self.hop_in.at[0], self.up)
-        self.b = self.net.send(hi, self.hop_in.at[1], self.down)
-
-    def above(self, lo, whole):
+        self.lo, self.hi, self.tail = lo, hi, []
+
+    def far(self, chunk):
+        self.a = self.net.send(chunk.at[self.lo], self.hop_in.at[0], self.up)
+        self.b = self.net.send(chunk.at[self.hi], self.hop_in.at[1], self.down)
+
+    def put(self, chunk, i, rows, way):
+        self.tail.append(self.net.send(chunk.at[rows], self.last_in.at[i].at[rows], way))
+
+    def above_now(self, chunk):
+        self.put(chunk, 0, self.hi, self.up)
+
+    def below_now(self, chunk):
+        self.put(chunk, 1, self.lo, self.down)
+
+    def above(self, chunk):
+        part = chunk.at[self.lo]
         self.a.wait_recv()
-        lo[...] = (lo[...].astype(F32) + self.hop_in[0].astype(F32)).astype(BF)
-        self.c = self.net.send(whole, self.last_in.at[0], self.up)
-
-    def below(self, hi, whole):
+        part[...] = (part[...].astype(F32) + self.hop_in[0].astype(F32)).astype(BF)
+        self.put(chunk, 0, self.lo, self.up)
+
+    def below(self, chunk):
+        part = chunk.at[self.hi]
         self.b.wait_recv()
-        hi[...] = (hi[...].astype(F32) + self.hop_in[1].astype(F32)).astype(BF)
-        self.d = self.net.send(whole, self.last_in.at[1], self.down)
+        part[...] = (part[...].astype(F32) + self.hop_in[1].astype(F32)).astype(BF)
+        self.put(chunk, 1, self.hi, self.down)
 
     def last(self, own):
         own = own.astype(F32)
-        self.c.wait_recv()
-        self.d.wait_recv()
+        for copy in self.tail:
+            copy.wait_recv()
         return own + self.last_in[0].astype(F32) + self.last_in[1].astype(F32)
 
 
 NT = (((1,), (1,)), ((), ()))
 TN = (((0,), (0,)), ((), ()))
-N_COPIES = 28 * 2 + 5 * 4 * 2 + 14 + 4 + 6 * 9 + 1 + 28 + 6
+N_COPIES = 40 * 2 + 7 * 4 * 2 + 14 + 4 + 6 * 9 + 1 + 42 + 6
 
 
 def kernel(
@@ -297,17 +328,18 @@
     cot = Gather(net, gf)
     cot.s1()
     xf = x_ref[...].astype(F32)
-    squares = row_sum(net, mine, got, jnp.sum(xf * xf, axis=1, keepdims=True))
-    inv = lax.rsqrt(squares / D + EPS)
+    squares = RowSum(net, mine, got, jnp.sum(xf * xf, axis=1, keepdims=True))
+    for copy in loads:
+        copy.wait()
+    wog[...] = (wo[...].astype(F32) * gate).astype(BF)
+    key_pos = jnp.concatenate([pos_ref[pl.ds(2 * g + h, 1), :] for h in range(2) for g in range(4)], axis=1)
+    for g in range(4):
+        pos_t[g] = jnp.broadcast_to(pos_ref[pl.ds(2 * g + k, 1), :], (128, HALF)).T
+    inv = lax.rsqrt(squares.total() / D + EPS)
     nf[y, z] = (xf * inv * (1.0 + scale) + shift).astype(BF)
     act = Gather(net, nf)
     act.s1()
-    for copy in loads:
-        copy.wait()
-    wog[...] = (wo[...].astype(F32) * gate).astype(BF)
-    key_pos = jnp.concatenate([pos_ref[pl.ds(0, 1), :], pos_ref[pl.ds(1, 1), :]], axis=1)
-    pos_t[...] = jnp.broadcast_to(pos_ref[pl.ds(k, 1), :], (128, 768)).T.reshape(4, HALF, 128)
-    order = (act.y, act.ym, act.yp, act.y2)
+    order = (y, (y + 3) % 4, (y + 1) % 4, (y + 2) % 4)
     rows_q = RowReduce(net, aq, pq, rq, hq, hqi, oq, iq, 384)
     rows_g = RowReduce(net, ag, pg, rg, hg, hgi, og, ig, 128)
 
@@ -348,41 +380,38 @@
     act.s2()
     act.s3()
     multiply(0)
-    act.s4a()
+    act.s4()
+    cot.s2()
     rows_q.r1(0)
-    act.s4b()
-    cot.s2()
-    act.zend("ym")
+    act.s5()
     multiply(1)
+    cot.s3()
     rows_q.r2(0)
-    act.zend("yp")
     multiply(2)
     rows_q.r1(1)
-    act.s5()
-    cot.s3()
+    act.s6()
+    cot.s4()
     multiply(3)
     rows_q.r1(2)
     rows_q.r2(1)
+    multiply_g(0)
+    cot.s5()
+    rows_q.r1(3)
     finish(0)
-    cot.s4a()
-    rows_q.r1(3)
     rows_q.r2(2)
-    cot.s4b()
+    multiply_g(1)
+    multiply_g(2)
+    cot.s6()
+    rows_q.r2(3)
+    rows_g.r1(0)
+    multiply_g(3)
     finish(1)
-    multiply_g(0)
-    rows_q.r2(3)
-    cot.zend("ym")
-    multiply_g(1)
-    rows_g.r1(0)
+    rows_g.r1(1)
+    rows_g.r1(2)
     finish(2)
-    cot.zend("yp")
-    multiply_g(2)
-    rows_g.r1(1)
+    rows_g.r2(0)
+    rows_g.r1(3)
     finish(3)
-    cot.s5()
-    multiply_g(3)
-    rows_g.r1(2)
-    rows_g.r2(0)
     rows_g.r2(1)
 
     groups = ((y + 2) % 4, (y + 1) % 4, (y + 3) % 4, y)
@@ -415,14 +444,14 @@
         grad_scores = (weights * (grad_probs - delta) * (inverse * factor)).astype(BF)
         r = jnp.dot(grad_scores, keys, preferred_element_type=F32)
         gpq[groups[s], k, :, pl.ds(384, 128)] = r.astype(BF)
-        grad_k = lax.dot_general(grad_scores, q, TN, preferred_element_type=F32)
-        grad_v = lax.dot_general(probs_b, g, TN, preferred_element_type=F32)
+        grad_k = jnp.dot(q.T, grad_scores, preferred_element_type=F32)
+        grad_v = jnp.dot(g.T, probs_b, preferred_element_type=F32)
         if s == 0:
-            dk[...] = grad_k.reshape(2, 768, 128)
-            dv[...] = grad_v.reshape(2, 768, 128)
+            dk[...] = grad_k
+            dv[...] = grad_v
         else:
-            dk[...] += grad_k.reshape(2, 768, 128)
-            dv[...] += grad_v.reshape(2, 768, 128)
+            dk[...] += grad_k
+            dv[...] += grad_v
 
     def gather_q(s):
         return RowGather(net, lambda rows, cols: gpq.at[groups[s], k, rows, cols], 128)
@@ -435,35 +464,27 @@
     context = RowGather(net, lambda rows, cols: cx.at[:, k, rows, cols], 128)
 
     attend(0)
-    rows_g.r1(3)
     rows_g.r2(2)
+    attend(1)
+    rows_g.r2(3)
     finish_g(0)
     finish_g(1)
-    attend(1)
-    rows_g.r2(3)
+    attend(2)
     finish_g(2)
-    attend(2)
     attend(3)
-    context.start()
     finish_g(3)
-    attend_grad(0)
-    moves_q[0].start()
-    context.forward()
-    attend_grad(1)
-    moves_q[1].start()
-    moves_q[0].forward()
-    context.finish()
-    attend_grad(2)
-    moves_q[2].start()
-    moves_q[1].forward()
-    moves_q[0].finish()
-    attend_grad(3)
-    part[:, pl.ds(0, 128)] = dk[1 - k].astype(BF)
-    part[:, pl.ds(128, 128)] = dv[1 - k].astype(BF)
+    for s in range(4):
+        attend_grad(s)
+        if s < 3:
+            moves_q[s].start()
+    mine_at = pl.ds(pl.multiple_of(k * 768, 128), 768)
+    theirs_at = pl.ds(pl.multiple_of((1 - k) * 768, 128), 768)
+    part[pl.ds(0, 128)] = dk[:, theirs_at].astype(BF)
+    part[pl.ds(128, 128)] = dv[:, theirs_at].astype(BF)
     swap = net.send(part, part_in, CORE)
     moves_q[3].start()
-    moves_q[2].forward()
-    moves_q[1].finish()
+    moves_q[0].forward()
+    moves_q[1].forward()
 
     stores = []
 
@@ -474,11 +495,11 @@
 
     heads = heads_of(x)
     head_at = [pl.ds(pl.multiple_of(head * 128, 128), 128) for head in heads]
-    ring_y0 = RingReduce(net, YP, YM, yh0, yi0)
-    rings_z1 = [RingReduce(net, ZP, ZM, zh1.at[s], zi1.at[s]) for s in range(4)]
-    ring_z0 = RingReduce(net, ZP, ZM, zh0, zi0)
-    ring_y1 = RingReduce(net, YP, YM, yh1, yi1)
     lo, hi = pl.ds(0, 48), pl.ds(48, 48)
+    ring_y0 = RingReduce(net, YP, YM, yh0, yi0, pl.ds(0, 2), pl.ds(2, 2))
+    rings_z1 = [RingReduce(net, ZP, ZM, zh1.at[s], zi1.at[s], lo, hi) for s in range(4)]
+    ring_z0 = RingReduce(net, ZP, ZM, zh0, zi0, lo, hi)
+    ring_y1 = RingReduce(net, YP, YM, yh1, yi1, lo, hi)
     zp, zm, z2 = (z + 1) % 4, (z + 3) % 4, (z + 2) % 4
 
     def normed_q(s):
@@ -521,70 +542,88 @@
         outq[rows, pl.ds(512, 1024)] = r.astype(BF)
 
     def z1_far(s):
-        rings_z1[s].far(gn.at[s, z2, lo, F1], gn.at[s, z2, hi, F1])
+        rings_z1[s].far(gn.at[s, z2, :, F1])
+        rings_z1[s].above_now(gn.at[s, zp, :, F1])
+        rings_z1[s].below_now(gn.at[s, zm, :, F1])
 
     def z1_near(s):
-        rings_z1[s].above(gn.at[s, zp, lo, F1], gn.at[s, zp, :, F1])
-        rings_z1[s].below(gn.at[s, zm, hi, F1], gn.at[s, zm, :, F1])
+        rings_z1[s].above(gn.at[s, zp, :, F1])
+        rings_z1[s].below(gn.at[s, zm, :, F1])
 
     def z1_last(s):
         return rings_z1[s].last(gn[s, z, :, F1])
 
+    def rows_of(s):
+        return gn.at[s, :, :, F0]
+
     swap.wait_recv()
-    for cols, total in ((pl.ds(0, 128), dk), (pl.ds(128, 128), dv)):
-        r = (total[k] + part_in[:, cols].astype(F32)).astype(BF)
-        gpkv[:, k, :, pl.ds(3 * 256 + cols.start, 128)] = r.reshape(4, HALF, 128)
+    for i, total in ((0, dk), (1, dv)):
+        r = total[:, mine_at] + part_in[pl.ds(i * 128, 128)].astype(F32)
+        gpkv[:, k, :, pl.ds(768 + i * 128, 128)] = r.T.astype(BF).reshape(4, HALF, 128)
     moves_kv[0].start()
+    moves_q[2].forward()
     moves_q[3].forward()
+    moves_kv[1].start()
+    moves_q[0].finish()
+    moves_q[1].finish()
+    normed_q(0)
     moves_q[2].finish()
-    moves_kv[1].start()
-    normed_q(0)
     moves_kv[0].forward()
+    moves_kv[2].start()
     moves_q[3].finish()
-    moves_kv[2].start()
     normed_q(1)
     normed_q(2)
     moves_kv[1].forward()
-    moves_kv[0].finish()
     moves_kv[3].start()
     normed_q(3)
-    gate_grad = out_weight()
+    moves_kv[0].finish()
+    weight_q(0)
     normed_kv(0)
-    ring_y0.far(gn.at[0, pl.ds(0, 2), :, F0], gn.at[0, pl.ds(2, 2), :, F0])
+    ring_y0.far(rows_of(0))
     z1_far(0)
     moves_kv[2].forward()
     moves_kv[1].finish()
+    weight_q(1)
     normed_kv(1)
+    ring_y0.above_now(rows_of(1))
     z1_far(1)
-    ring_y0.above(gn.at[1, pl.ds(0, 2), :, F0], gn.at[1, :, :, F0])
+    moves_kv[3].forward()
+    context.start()
+    moves_kv[2].finish()
     z1_near(0)
-    moves_kv[3].forward()
-    moves_kv[2].finish()
     normed_kv(2)
+    ring_y0.below_now(rows_of(2))
     z1_far(2)
-    ring_y0.below(gn.at[2, pl.ds(2, 2), :, F0], gn.at[2, :, :, F0])
+    ring_y0.above(rows_of(1))
+    moves_kv[3].finish()
+    context.forward()
     z1_near(1)
-    t1[0] = z1_last(0).astype(BF)
-    ring_y1.far(t1.at[0, lo], t1.at[0, hi])
-    moves_kv[3].finish()
-    weight_q(0)
-    weight_q(1)
     normed_kv(3)
     z1_far(3)
+    ring_y0.below(rows_of(2))
+    t1[0] = z1_last(0).astype(BF)
+    ring_y1.far(t1.at[0])
     z1_near(2)
     t1[1] = z1_last(1).astype(BF)
-    ring_y1.above(t1.at[1, lo], t1.at[1])
+    ring_y1.above_now(t1.at[1])
+    z1_near(3)
+    weight_q(2)
+    ring_y1.above(t1.at[1])
+    t1[2] = z1_last(2).astype(BF)
+    ring_y1.below_now(t1.at[2])
+    ring_y1.below(t1.at[2])
+    context.finish()
+    weight_q(3)
     t0[...] = ring_y0.last(gn[3, :, :, F0]).astype(BF)
-    ring_z0.far(t0.at[z2, lo], t0.at[z2, hi])
-    z1_near(3)
-    t1[2] = z1_last(2).astype(BF)
-    ring_y1.below(t1.at[2, hi], t1.at[2])
-    weight_q(2)
-    ring_z0.above(t0.at[zp, lo], t0.at[zp])
-    ring_z0.below(t0.at[zm, hi], t0.at[zm])
-    weight_q(3)
+    ring_z0.far(t0.at[z2])
+    ring_z0.above_now(t0.at[zp])
+    ring_z0.below_now(t0.at[zm])
+    gate_grad = out_weight()
+    ring_z0.above(t0.at[zp])
+    ring_z0.below(t0.at[zm])
     t1[3] = z1_last(3).astype(BF)
     weight_kv(0)
+    weight_kv(1)
 
     grad0 = ring_z0.last(t0[z])
     grad1 = ring_y1.last(t1[3])
@@ -597,18 +636,19 @@
     sums[0, pl.ds(3, 5)] = jnp.zeros((5, 1024), F32)
     sums_z[z] = sums[0]
     zc = [net.send(sums.at[0], sums_z.at[z], step) for step in (ZP, ZM, Z2)]
-    inner = row_sum(net, mine2, got2, jnp.sum(grad_hat * x_hat, axis=1, keepdims=True)) / D
+    inner = RowSum(net, mine2, got2, jnp.sum(grad_hat * x_hat, axis=1, keepdims=True))
+    weight_kv(2)
+    weight_kv(3)
+    for d in range(4):
+        for j, place in enumerate((d * 128, 512 + d * 256, 640 + d * 256)):
+            store(outq.at[:, pl.ds(place, 128)], gqkv.at[j, :, head_at[d]])
     for copy in zc:
         copy.wait_recv()
     sums[1] = (sums_z[0] + sums_z[1]) + (sums_z[2] + sums_z[3])
     sums_y[y] = sums[1]
     yc = [net.send(sums.at[1], sums_y.at[y], step) for step in (YP, YM, Y2)]
+    inner = inner.total() / D
     gin[...] = ((grad_hat - x_hat * inner) * inv + gout_ref[...].astype(F32)).astype(BF)
-    for m in range(1, 4):
-        weight_kv(m)
-    for d in range(4):
-        for j, place in enumerate((d * 128, 512 + d * 256, 640 + d * 256)):
-            store(outq.at[:, pl.ds(place, 128)], gqkv.at[j, :, head_at[d]])
     for copy in yc:
         copy.wait_recv()
     gmod[...] = ((sums_y[0] + sums_y[1]) + (sums_y[2] + sums_y[3]))[0:3]
@@ -617,6 +657,28 @@
         copy.wait()
 
 
+def place_kernel(a, b, c, d, oa, ob, oc, od, va, vb_, vc, vd, load_sem, store_sem):
+    parts = []
+    for src, mid, dst, n in ((a, va, oa, 1), (b, vb_, ob, 1), (c, vc, oc, 6), (d, vd, od, 2)):
+        for i in range(n):
+            if n == 6:
+                at = (i // 2, pl.ds(512 * (i % 2), 512))
+            elif n == 2:
+                at = (pl.ds(256 * i, 256),)
+            else:
+                at = (slice(None),)
+            parts.append((src.at[at], mid.at[at], dst.at[at]))
+    loads = [pltpu.make_async_copy(p[0], p[1], load_sem.at[i]) for i, p in enumerate(parts)]
+    puts = [pltpu.make_async_copy(p[1], p[2], store_sem.at[i]) for i, p in enumerate(parts)]
+    for copy in loads:
+        copy.start()
+    for load, put in zip(loads, puts):
+        load.wait()
+        put.start()
+    for copy in puts:
+        copy.wait()
+
+
 VM = pl.BlockSpec(memory_space=pltpu.VMEM)
 SM = pl.BlockSpec(memory_space=pltpu.SMEM)
 ANY = pl.BlockSpec(memory_space=pl.ANY)
@@ -637,7 +699,7 @@
 def shards(block_input, modulation, iteration, positions, qkv_weight, out_weight, grad_out):
     mod = modulation.transpose(1, 0, 2)
     wq = qkv_weight.transpose(1, 0, 2)
-    pos = positions.astype(F32).reshape(4, 2, HALF).transpose(1, 0, 2).reshape(2, 768)
+    pos = positions.reshape(8, HALF)
 
     def rows(w):
         return [
@@ -655,8 +717,8 @@
             vb(4, 4, 96, 1024), vb(4, 4, 96, 1024), vb(4, HALF, 256),
             vb(1024, 1536), vb(512, 1024), vb(512, 1024),
             *rows(384), *rows(128), vf(8, 128), vf(7, 8, 128), vf(8, 128), vf(7, 8, 128),
-            vb(2, 4, HALF, 256), vf(4, HALF, 1536), vf(4, HALF, 128), vf(4, HALF, 128),
-            vf(2, 768, 128), vf(2, 768, 128), vb(768, 256), vb(768, 256),
+            vb(2, 4, HALF, 256), vf(4, HALF, 1536), pltpu.VMEM((4, HALF, 128), jnp.int32), vf(4, HALF, 128),
+            vf(128, 1536), vf(128, 1536), vb(256, 768), vb(256, 768),
             vb(4, 2, HALF, 512), vb(4, 2, HALF, 1024), vb(4, 2, HALF, 512),
             vf(4, 384, 1024), vb(4, 4, 96, 1024),
             vb(2, 2, 96, 512), vb(2, 4, 96, 512), vb(4, 96, 512), vb(2, 48, 512), vb(2, 96, 512),
@@ -669,6 +731,18 @@
             collective_id=0, has_side_effects=True, vmem_limit_bytes=63 << 20
         ),
     )(block_input, grad_out, mod, iteration, pos, wq, out_weight)
+    shapes = [(96, 1024), (3, 1024), (3, 1024, 512), (512, 1024)]
+    types = [BF, F32, BF, BF]
+    gin, gmod, gqkv, gow = pl.pallas_call(
+        place_kernel,
+        name="place",
+        out_shape=[sds(a, b) for a, b in zip(shapes, types)],
+        in_specs=[ANY] * 4,
+        out_specs=[ANY] * 4,
+        scratch_shapes=[pltpu.VMEM(a, b) for a, b in zip(shapes, types)]
+        + [pltpu.SemaphoreType.DMA((10,)), pltpu.SemaphoreType.DMA((10,))],
+        compiler_params=pltpu.CompilerParams(vmem_limit_bytes=63 << 20),
+    )(gin, gmod, gqkv, gow)
     return gin, gqkv.transpose(1, 0, 2), gow, gmod
 
 

time: 152 us -> 132 us (0.87)
  Pallas kernels: 141 us -> 129 us
  local copies, waits for them, and re-layouts: 7.81 us -> 1.37 us
    pallas_call x1, Pallas kernels: 141 us -> 125 us  [shards(): pl.pallas_call(kernel, name='block_backward', out_shape=(sds((96, 1024)),...]
    unnamed x8 -> x0, local copies, waits for them, and re-layouts: 7.04 us -> none
    pallas_call x0 -> x1, Pallas kernels: none -> 3.98 us  [shards(): pl.pallas_call(place_kernel, name='place', out_shape=[sds(a, b) for a, b...]
where the time goes in v3:
time: 132 us
  Pallas kernels  129 us (98%)
  between operations  1.47 us (1%)
  local copies, waits for them, and re-layouts  1.37 us (1%)
    pallas_call x1, Pallas kernels, shards(): pl.pallas_call(kernel, name='block_backward', out_shape=(sds((96, 1024)),...  125 us
    pallas_call x1, Pallas kernels, shards(): pl.pallas_call(place_kernel, name='place', out_shape=[sds(a, b) for a, b...  3.98 us

profile of v3, /device:TPU:0, one launch (start us, length us, event | category | flops | bytes accessed | tf_op | source)
XLA Modules:
  0.0 132.1 jit_solution(955320706779299042)
XLA Ops:
  1.3 1.4 %reshape.11.pos_ref = s32[8,192]{1,0:T(8,128)} reshape(s32[1536]{0:T(1024)} %param.10) | data formatting | bytes 12288 | tf_op jit(solution)/shard_map/reshape | solution.py:702
  2.6 125.3 %block_backward.1 = (bf16[96,1024]{1,0:T(8,128)(2,1)}, f32[3,1024]{1,0:T(4,128)}, bf16[3,1024,512]{2,1,0:T(8,128)(2,1)}, bf16[512,1024]{1,0:T(8,128)(2,1)}) custom-call(bf16[96,1024]{1,0:T(8,128)(2,1)} %x_ref.1, bf16[96,1024]{1,0:T(8,128)(2,1)} %gout_ref.1, f32[3,8,1024]{2,1,0:T(8,128)} %bitcast.4, s32[1]{0:T(128)S(6)} %copy.11.it_ref, ...), custom_call_target="tpu_custom_call" | custom-call | tf_op jit(solution)/shard_map/block_backward/pallas_call | solution.py:710
  128.0 4.0 %place.1 = (bf16[96,1024]{1,0:T(8,128)(2,1)}, f32[3,1024]{1,0:T(4,128)}, bf16[3,1024,512]{2,1,0:T(8,128)(2,1)}, bf16[512,1024]{1,0:T(8,128)(2,1)}) custom-call(bf16[96,1024]{1,0:T(8,128)(2,1)} %get-tuple-element.12.a, f32[3,1024]{1,0:T(4,128)} %get-tuple-element.13.b, bf16[3,1024,512]{2,1,0:T(8,128)(2,1)} %get-tuple-element.14.c, ...), custom_call_target="tpu_custom_call" | custom-call | tf_op jit(solution)/shard_map/place/pallas_call | solution.py:736

commit v4 on v3

--- a/solution.py
+++ b/solution.py
@@ -22,6 +22,7 @@
 G = 4
 HALF = 192
 F0, F1 = pl.ds(0, 512), pl.ds(512, 512)
+R0, R1 = pl.ds(0, 384), pl.ds(384, 640)
 
 
 def coords():
@@ -329,12 +330,11 @@
     cot.s1()
     xf = x_ref[...].astype(F32)
     squares = RowSum(net, mine, got, jnp.sum(xf * xf, axis=1, keepdims=True))
-    for copy in loads:
-        copy.wait()
-    wog[...] = (wo[...].astype(F32) * gate).astype(BF)
-    key_pos = jnp.concatenate([pos_ref[pl.ds(2 * g + h, 1), :] for h in range(2) for g in range(4)], axis=1)
+    pos = [[pos_ref[:, pl.ds(g * 384 + h * HALF, HALF)] for g in range(4)] for h in range(2)]
+    key_pos = jnp.concatenate(pos[0] + pos[1], axis=1)
     for g in range(4):
-        pos_t[g] = jnp.broadcast_to(pos_ref[pl.ds(2 * g + k, 1), :], (128, HALF)).T
+        own_pos = jnp.where(k == 0, pos[0][g], pos[1][g])
+        pos_t[g] = jnp.broadcast_to(own_pos, (128, HALF)).T
     inv = lax.rsqrt(squares.total() / D + EPS)
     nf[y, z] = (xf * inv * (1.0 + scale) + shift).astype(BF)
     act = Gather(net, nf)
@@ -378,6 +378,8 @@
         qkvg[order[s], :, pl.ds(128, 128)] = rows_g.r3(s)
 
     act.s2()
+    for copy in loads:
+        copy.wait()
     act.s3()
     multiply(0)
     act.s4()
@@ -394,24 +396,25 @@
     multiply(3)
     rows_q.r1(2)
     rows_q.r2(1)
+    wog[...] = (wo[...].astype(F32) * gate).astype(BF)
+    rows_q.r1(3)
+    cot.s5()
+    rows_q.r2(2)
     multiply_g(0)
-    cot.s5()
-    rows_q.r1(3)
+    multiply_g(1)
     finish(0)
-    rows_q.r2(2)
-    multiply_g(1)
-    multiply_g(2)
-    cot.s6()
     rows_q.r2(3)
     rows_g.r1(0)
+    multiply_g(2)
+    rows_g.r1(1)
+    finish(1)
+    cot.s6()
     multiply_g(3)
-    finish(1)
-    rows_g.r1(1)
+    finish(2)
     rows_g.r1(2)
-    finish(2)
     rows_g.r2(0)
+    finish(3)
     rows_g.r1(3)
-    finish(3)
     rows_g.r2(1)
 
     groups = ((y + 2) % 4, (y + 1) % 4, (y + 3) % 4, y)
@@ -446,7 +449,7 @@
         gpq[groups[s], k, :, pl.ds(384, 128)] = r.astype(BF)
         grad_k = jnp.dot(q.T, grad_scores, preferred_element_type=F32)
         grad_v = jnp.dot(g.T, probs_b, preferred_element_type=F32)
-        if s == 0:
+        if s == 3:
             dk[...] = grad_k
             dv[...] = grad_v
         else:
@@ -466,25 +469,20 @@
     attend(0)
     rows_g.r2(2)
     attend(1)
+    attend(2)
     rows_g.r2(3)
-    finish_g(0)
-    finish_g(1)
-    attend(2)
-    finish_g(2)
     attend(3)
-    finish_g(3)
-    for s in range(4):
-        attend_grad(s)
-        if s < 3:
-            moves_q[s].start()
+    for i in range(4):
+        finish_g(i)
+        attend_grad(3 - i)
+        if i < 3:
+            moves_q[3 - i].start()
     mine_at = pl.ds(pl.multiple_of(k * 768, 128), 768)
     theirs_at = pl.ds(pl.multiple_of((1 - k) * 768, 128), 768)
     part[pl.ds(0, 128)] = dk[:, theirs_at].astype(BF)
     part[pl.ds(128, 128)] = dv[:, theirs_at].astype(BF)
     swap = net.send(part, part_in, CORE)
-    moves_q[3].start()
-    moves_q[0].forward()
-    moves_q[1].forward()
+    moves_q[0].start()
 
     stores = []
 
@@ -542,47 +540,45 @@
         outq[rows, pl.ds(512, 1024)] = r.astype(BF)
 
     def z1_far(s):
-        rings_z1[s].far(gn.at[s, z2, :, F1])
-        rings_z1[s].above_now(gn.at[s, zp, :, F1])
-        rings_z1[s].below_now(gn.at[s, zm, :, F1])
+        rings_z1[s].far(gn.at[s, z2, :, R1])
+        rings_z1[s].above_now(gn.at[s, zp, :, R1])
+        rings_z1[s].below_now(gn.at[s, zm, :, R1])
 
     def z1_near(s):
-        rings_z1[s].above(gn.at[s, zp, :, F1])
-        rings_z1[s].below(gn.at[s, zm, :, F1])
+        rings_z1[s].above(gn.at[s, zp, :, R1])
+        rings_z1[s].below(gn.at[s, zm, :, R1])
 
     def z1_last(s):
-        return rings_z1[s].last(gn[s, z, :, F1])
+        return rings_z1[s].last(gn[s, z, :, R1])
 
     def rows_of(s):
-        return gn.at[s, :, :, F0]
+        return gn.at[s, :, :, R0]
 
     swap.wait_recv()
     for i, total in ((0, dk), (1, dv)):
         r = total[:, mine_at] + part_in[pl.ds(i * 128, 128)].astype(F32)
         gpkv[:, k, :, pl.ds(768 + i * 128, 128)] = r.T.astype(BF).reshape(4, HALF, 128)
     moves_kv[0].start()
-    moves_q[2].forward()
-    moves_q[3].forward()
     moves_kv[1].start()
-    moves_q[0].finish()
-    moves_q[1].finish()
-    normed_q(0)
-    moves_q[2].finish()
+    for s in (3, 2, 1, 0):
+        moves_q[s].forward()
     moves_kv[0].forward()
     moves_kv[2].start()
-    moves_q[3].finish()
-    normed_q(1)
-    normed_q(2)
+    for s in (3, 2, 1, 0):
+        moves_q[s].finish()
     moves_kv[1].forward()
     moves_kv[3].start()
+    normed_q(0)
+    normed_q(1)
+    moves_kv[0].finish()
+    normed_q(2)
     normed_q(3)
-    moves_kv[0].finish()
-    weight_q(0)
     normed_kv(0)
     ring_y0.far(rows_of(0))
     z1_far(0)
     moves_kv[2].forward()
     moves_kv[1].finish()
+    weight_q(0)
     weight_q(1)
     normed_kv(1)
     ring_y0.above_now(rows_of(1))
@@ -591,12 +587,12 @@
     context.start()
     moves_kv[2].finish()
     z1_near(0)
+    weight_q(2)
     normed_kv(2)
     ring_y0.below_now(rows_of(2))
     z1_far(2)
+    moves_kv[3].finish()
     ring_y0.above(rows_of(1))
-    moves_kv[3].finish()
-    context.forward()
     z1_near(1)
     normed_kv(3)
     z1_far(3)
@@ -604,26 +600,26 @@
     t1[0] = z1_last(0).astype(BF)
     ring_y1.far(t1.at[0])
     z1_near(2)
+    context.forward()
     t1[1] = z1_last(1).astype(BF)
     ring_y1.above_now(t1.at[1])
+    weight_q(3)
     z1_near(3)
-    weight_q(2)
+    t0[...] = ring_y0.last(gn[3, :, :, R0]).astype(BF)
+    ring_z0.far(t0.at[z2])
+    ring_z0.above_now(t0.at[zp])
+    ring_z0.below_now(t0.at[zm])
     ring_y1.above(t1.at[1])
     t1[2] = z1_last(2).astype(BF)
     ring_y1.below_now(t1.at[2])
     ring_y1.below(t1.at[2])
     context.finish()
-    weight_q(3)
-    t0[...] = ring_y0.last(gn[3, :, :, F0]).astype(BF)
-    ring_z0.far(t0.at[z2])
-    ring_z0.above_now(t0.at[zp])
-    ring_z0.below_now(t0.at[zm])
-    gate_grad = out_weight()
+    weight_kv(0)
+    weight_kv(1)
     ring_z0.above(t0.at[zp])
     ring_z0.below(t0.at[zm])
+    gate_grad = out_weight()
     t1[3] = z1_last(3).astype(BF)
-    weight_kv(0)
-    weight_kv(1)
 
     grad0 = ring_z0.last(t0[z])
     grad1 = ring_y1.last(t1[3])
@@ -699,7 +695,7 @@
 def shards(block_input, modulation, iteration, positions, qkv_weight, out_weight, grad_out):
     mod = modulation.transpose(1, 0, 2)
     wq = qkv_weight.transpose(1, 0, 2)
-    pos = positions.reshape(8, HALF)
+    pos = positions.reshape(1, 1536)
 
     def rows(w):
         return [
@@ -721,8 +717,8 @@
             vf(128, 1536), vf(128, 1536), vb(256, 768), vb(256, 768),
             vb(4, 2, HALF, 512), vb(4, 2, HALF, 1024), vb(4, 2, HALF, 512),
             vf(4, 384, 1024), vb(4, 4, 96, 1024),
-            vb(2, 2, 96, 512), vb(2, 4, 96, 512), vb(4, 96, 512), vb(2, 48, 512), vb(2, 96, 512),
-            vb(4, 2, 48, 512), vb(4, 2, 96, 512), vb(4, 96, 512), vb(2, 48, 512), vb(2, 96, 512),
+            vb(2, 2, 96, 384), vb(2, 4, 96, 384), vb(4, 96, 384), vb(2, 48, 384), vb(2, 96, 384),
+            vb(4, 2, 48, 640), vb(4, 2, 96, 640), vb(4, 96, 640), vb(2, 48, 640), vb(2, 96, 640),
             vb(1024, 1536), vb(512, 1024), vf(2, 8, 1024), vf(4, 8, 1024), vf(4, 8, 1024),
             pltpu.SemaphoreType.DMA((N_COPIES,)), pltpu.SemaphoreType.DMA((N_COPIES,)),
             pltpu.SemaphoreType.DMA((16,)), pltpu.SemaphoreType.DMA((16,)),

time: 132 us -> 127 us (0.962)
  Pallas kernels: 129 us -> 124 us
    pallas_call x1, Pallas kernels: 125 us -> 120 us  [shards(): pl.pallas_call(kernel, name='block_backward', out_shape=(sds((96, 1024)),...]
where the time goes in v4:
time: 127 us
  Pallas kernels  124 us (98%)
  between operations  1.47 us (1%)
  local copies, waits for them, and re-layouts  1.3 us (1%)
    pallas_call x1, Pallas kernels, shards(): pl.pallas_call(kernel, name='block_backward', out_shape=(sds((96, 1024)),...  120 us
    pallas_call x1, Pallas kernels, shards(): pl.pallas_call(place_kernel, name='place', out_shape=[sds(a, b) for a, b...  3.98 us

profile of v4, /device:TPU:0, one launch (start us, length us, event | category | flops | bytes accessed | tf_op | source)
XLA Modules:
  0.0 127.1 jit_solution(4187235566155575033)
XLA Ops:
  1.3 1.3 %reshape.11.pos_ref = s32[1,1536]{1,0:T(1,128)} reshape(s32[1536]{0:T(1024)} %param.10) | data formatting | bytes 12288 | tf_op jit(solution)/shard_map/reshape | solution.py:698
  2.6 120.3 %block_backward.1 = (bf16[96,1024]{1,0:T(8,128)(2,1)}, f32[3,1024]{1,0:T(4,128)}, bf16[3,1024,512]{2,1,0:T(8,128)(2,1)}, bf16[512,1024]{1,0:T(8,128)(2,1)}) custom-call(bf16[96,1024]{1,0:T(8,128)(2,1)} %x_ref.1, bf16[96,1024]{1,0:T(8,128)(2,1)} %gout_ref.1, f32[3,8,1024]{2,1,0:T(8,128)} %bitcast.4, s32[1]{0:T(128)S(6)} %copy.11.it_ref, ...), custom_call_target="tpu_custom_call" | custom-call | tf_op jit(solution)/shard_map/block_backward/pallas_call | solution.py:706
  122.9 4.0 %place.1 = (bf16[96,1024]{1,0:T(8,128)(2,1)}, f32[3,1024]{1,0:T(4,128)}, bf16[3,1024,512]{2,1,0:T(8,128)(2,1)}, bf16[512,1024]{1,0:T(8,128)(2,1)}) custom-call(bf16[96,1024]{1,0:T(8,128)(2,1)} %get-tuple-element.12.a, f32[3,1024]{1,0:T(4,128)} %get-tuple-element.13.b, bf16[3,1024,512]{2,1,0:T(8,128)(2,1)} %get-tuple-element.14.c, ...), custom_call_target="tpu_custom_call" | custom-call | tf_op jit(solution)/shard_map/place/pallas_call | solution.py:732

commit v5 on v4

--- a/solution.py
+++ b/solution.py
@@ -383,34 +383,34 @@
     act.s3()
     multiply(0)
     act.s4()
-    cot.s2()
     rows_q.r1(0)
     act.s5()
     multiply(1)
-    cot.s3()
     rows_q.r2(0)
+    cot.s2()
     multiply(2)
     rows_q.r1(1)
     act.s6()
+    rows_q.r1(2)
+    multiply(3)
+    rows_q.r2(1)
+    cot.s3()
+    rows_q.r2(2)
+    rows_q.r1(3)
     cot.s4()
-    multiply(3)
-    rows_q.r1(2)
-    rows_q.r2(1)
     wog[...] = (wo[...].astype(F32) * gate).astype(BF)
-    rows_q.r1(3)
+    finish(0)
     cot.s5()
-    rows_q.r2(2)
+    rows_q.r2(3)
     multiply_g(0)
     multiply_g(1)
-    finish(0)
-    rows_q.r2(3)
+    finish(1)
     rows_g.r1(0)
     multiply_g(2)
     rows_g.r1(1)
-    finish(1)
+    finish(2)
     cot.s6()
     multiply_g(3)
-    finish(2)
     rows_g.r1(2)
     rows_g.r2(0)
     finish(3)

time: 127 us -> 123 us (0.969)
  Pallas kernels: 124 us -> 120 us
    pallas_call x1, Pallas kernels: 120 us -> 116 us  [shards(): pl.pallas_call(kernel, name='block_backward', out_shape=(sds((96, 1024)),...]
where the time goes in v5:
time: 123 us
  Pallas kernels  120 us (98%)
  between operations  1.47 us (1%)
  local copies, waits for them, and re-layouts  1.3 us (1%)
    pallas_call x1, Pallas kernels, shards(): pl.pallas_call(kernel, name='block_backward', out_shape=(sds((96, 1024)),...  116 us
    pallas_call x1, Pallas kernels, shards(): pl.pallas_call(place_kernel, name='place', out_shape=[sds(a, b) for a, b...  3.98 us

profile of v5, /device:TPU:0, one launch (start us, length us, event | category | flops | bytes accessed | tf_op | source)
XLA Modules:
  0.0 123.2 jit_solution(7044066652668064875)
XLA Ops:
  1.3 1.3 %reshape.11.pos_ref = s32[1,1536]{1,0:T(1,128)} reshape(s32[1536]{0:T(1024)} %param.10) | data formatting | bytes 12288 | tf_op jit(solution)/shard_map/reshape | solution.py:698
  2.6 116.4 %block_backward.1 = (bf16[96,1024]{1,0:T(8,128)(2,1)}, f32[3,1024]{1,0:T(4,128)}, bf16[3,1024,512]{2,1,0:T(8,128)(2,1)}, bf16[512,1024]{1,0:T(8,128)(2,1)}) custom-call(bf16[96,1024]{1,0:T(8,128)(2,1)} %x_ref.1, bf16[96,1024]{1,0:T(8,128)(2,1)} %gout_ref.1, f32[3,8,1024]{2,1,0:T(8,128)} %bitcast.4, s32[1]{0:T(128)S(6)} %copy.11.it_ref, ...), custom_call_target="tpu_custom_call" | custom-call | tf_op jit(solution)/shard_map/block_backward/pallas_call | solution.py:706
  119.0 4.0 %place.1 = (bf16[96,1024]{1,0:T(8,128)(2,1)}, f32[3,1024]{1,0:T(4,128)}, bf16[3,1024,512]{2,1,0:T(8,128)(2,1)}, bf16[512,1024]{1,0:T(8,128)(2,1)}) custom-call(bf16[96,1024]{1,0:T(8,128)(2,1)} %get-tuple-element.12.a, f32[3,1024]{1,0:T(4,128)} %get-tuple-element.13.b, bf16[3,1024,512]{2,1,0:T(8,128)(2,1)} %get-tuple-element.14.c, ...), custom_call_target="tpu_custom_call" | custom-call | tf_op jit(solution)/shard_map/place/pallas_call | solution.py:732
